TPU v7x, 128 devices: a whole 4x4x4 slice. The times are simulated.
128 devices in a mesh: ctx: 16 (over x_lo, y, core), ch: 8 (over x_hi, z).
Axes of the slice: x: 4 (x_hi: 2, x_lo: 2; x = x_hi * 2 + x_lo), y: 4, z: 4, core: 2. Of those that a mesh axis runs over, the one named last changes fastest.
Arguments:
- query_branch: bfloat16 [4096, 8192], P('ctx', 'ch'), may hold values from -6 to 6
- key_raw: bfloat16 [4096, 8192], P('ctx', 'ch'), may hold values from -6 to 6
- value_branch: bfloat16 [4096, 8192], P('ctx', 'ch'), may hold values from -6 to 6
- conv_out: bfloat16 [4096, 8192], P('ctx', 'ch'), may hold values from -6 to 6
- out_grad: bfloat16 [4096, 8192], P('ctx', 'ch'), may hold values from -18 to 18
- long_filter: bfloat16 [4096, 8192], P('ctx', 'ch'), may hold values from -0.09375 to 0.09375
- short_filter: float32 [3, 8192], P(None, 'ch'), may hold values from -3 to 3
Outputs:
- query_grad: bfloat16 [4096, 8192], P('ctx', 'ch')
- key_raw_grad: bfloat16 [4096, 8192], P('ctx', 'ch')
- value_grad: bfloat16 [4096, 8192], P('ctx', 'ch')
- filter_grad: float32 [4096, 8192], P('ctx', 'ch')
- short_grad: float32 [3, 8192], P(None, 'ch')
All inputs are finite; a program needn't handle non-finite values.
Results may differ from a plain program's by a relative error of at most 0.0049.
Values may be sent and summed in bfloat16 or wider, within the bound.
A program may use at most 128 MiB of HBM per device.

v0:
```python
import math

import jax
import jax.numpy as jnp
from jax import lax
from jax.sharding import PartitionSpec as P

HIGHEST = lax.Precision.HIGHEST


def shifted(block, axis, distance):
    devices = range(lax.axis_size(axis))
    route = [(i - distance, i) for i in devices if i - distance in devices]
    return lax.ppermute(block, axis, route)


def spectral_tables(block_rows):
    length = 2 * block_rows
    rows_all = jnp.arange(length, dtype=jnp.int32)
    frequency = jnp.where(rows_all <= block_rows, rows_all, rows_all - block_rows)
    cosine_rows = rows_all <= block_rows
    column = jnp.arange(block_rows, dtype=jnp.int32)
    phase_index = frequency[:, None] * column[None, :] % length
    angles = phase_index.astype(jnp.float32) * (math.pi / block_rows)
    forward_table = jnp.where(cosine_rows[:, None], jnp.cos(angles), -jnp.sin(angles))
    upper = lax.optimization_barrier(forward_table.astype(jnp.bfloat16))
    lower = (forward_table - upper.astype(jnp.float32)).astype(jnp.bfloat16)
    forward_pair = jnp.concatenate([upper, lower], axis=1)
    edge = (frequency == 0) | (frequency == block_rows)
    weight = jnp.where(edge, 1.0, 2.0).astype(jnp.float32) / length
    inverse_table = forward_table.T * weight[None, :]
    parity = jnp.where(frequency % 2 == 0, 1.0, -1.0).astype(jnp.float32)[:, None]
    dc_mask = jnp.where(column == 0, 0.0, 1.0).astype(jnp.float32)[:, None]
    return (forward_pair, inverse_table, parity, dc_mask)


def forward(forward_pair, data_block):
    doubled = jnp.concatenate([data_block, data_block], axis=0)
    return jnp.dot(forward_pair, doubled, preferred_element_type=jnp.float32)


def conj_product(left, right, dc_mask):
    half = left.shape[0] // 2
    left_re, left_im = (left[:half], left[half:])
    right_re, right_im = (right[:half], right[half:])
    both_im = left_im * right_im
    real_part = left_re * right_re + dc_mask * both_im
    imag_part = dc_mask * (left_re * right_im - left_im * right_re) + (1.0 - dc_mask) * both_im
    return jnp.concatenate([real_part, imag_part], axis=0)


def sequence_blocks(long_filter, gated, conv_grad, tables):
    forward_pair, inverse_table, parity, dc_mask = tables
    block_rows, local_width = gated.shape
    block_count = lax.axis_size("ctx")
    filters = lax.all_gather(long_filter, "ctx", axis=0, tiled=True)
    gateds = lax.all_gather(gated, "ctx", axis=0, tiled=True)
    spectrum_zero = jnp.zeros((2 * block_rows, local_width), jnp.float32)

    def pair_step(turn_index, carried, grad_block):
        out_acc, lag_acc, prev_filter, prev_gated = carried
        row_start = turn_index * block_rows
        filter_block = lax.dynamic_slice_in_dim(filters, row_start, block_rows, 0)
        gated_block = lax.dynamic_slice_in_dim(gateds, row_start, block_rows, 0)
        spectra = forward(
            forward_pair, jnp.concatenate([filter_block, gated_block, grad_block], axis=1)
        )
        filter_spec = spectra[:, :local_width]
        gated_spec = spectra[:, local_width : 2 * local_width]
        grad_spec = spectra[:, 2 * local_width :]
        out_acc = out_acc + conj_product(filter_spec + parity * prev_filter, grad_spec, dc_mask)
        lag_acc = lag_acc + conj_product(gated_spec + parity * prev_gated, grad_spec, dc_mask)
        return (out_acc, lag_acc, filter_spec, gated_spec)

    initial = (spectrum_zero, spectrum_zero, spectrum_zero, spectrum_zero)

    def cycle_turn(turn_index, status):
        carried, held = status
        carried = pair_step(turn_index, carried, held)
        held = shifted(held, "ctx", -1)
        return (carried, held)

    carried, held = lax.fori_loop(0, block_count - 1, cycle_turn, (initial, conv_grad))
    carried = pair_step(block_count - 1, carried, held)
    out_acc, lag_acc = (carried[0], carried[1])
    paired = jnp.dot(
        inverse_table,
        jnp.concatenate([out_acc, lag_acc], axis=1),
        precision=HIGHEST,
        preferred_element_type=jnp.float32,
    )
    return (paired[:, :local_width], paired[:, local_width:])


def per_device(query_branch, key_raw, value_branch, conv_out, out_grad, long_filter, short_filter):
    block_rows, local_width = query_branch.shape
    tap_count = short_filter.shape[0]
    block_count = lax.axis_size("ctx")
    tables = spectral_tables(block_rows)
    before = shifted(key_raw[block_rows - (tap_count - 1) :], "ctx", 1)
    extended = jnp.concatenate([before, key_raw], axis=0).astype(jnp.float32)
    key_conv = jnp.zeros((block_rows, local_width), jnp.float32)
    for shift_tap in range(tap_count):
        key_conv = (
            key_conv
            + short_filter[shift_tap]
            * extended[tap_count - 1 - shift_tap : tap_count - 1 - shift_tap + block_rows]
        )
    value_wide = value_branch.astype(jnp.float32)
    gated = (key_conv * value_wide).astype(jnp.bfloat16)
    grad_wide = out_grad.astype(jnp.float32)
    query_grad = (grad_wide * conv_out.astype(jnp.float32)).astype(jnp.bfloat16)
    conv_grad = (grad_wide * query_branch.astype(jnp.float32)).astype(jnp.bfloat16)
    gated_grad, lag_grad = sequence_blocks(long_filter, gated, conv_grad, tables)
    value_grad = (gated_grad * key_conv).astype(jnp.bfloat16)
    key_grad = gated_grad * value_wide
    rows_next = shifted(key_grad[: tap_count - 1], "ctx", -1)
    tail_ext = jnp.concatenate([key_grad, rows_next], axis=0)
    raw_total = jnp.zeros((block_rows, local_width), jnp.float32)
    for shift_tap in range(tap_count):
        raw_total = (
            raw_total + short_filter[shift_tap] * tail_ext[shift_tap : shift_tap + block_rows]
        )
    key_raw_grad = raw_total.astype(jnp.bfloat16)
    tap_terms = jnp.stack(
        [
            jnp.sum(
                key_grad
                * extended[tap_count - 1 - shift_tap : tap_count - 1 - shift_tap + block_rows],
                axis=0,
            )
            for shift_tap in range(tap_count)
        ]
    )
    short_grad = lax.psum(tap_terms, "ctx")
    squares = jnp.sum(lag_grad * lag_grad)
    total_squares = lax.psum(squares, ("ctx", "ch"))
    entries = float(block_rows * local_width * block_count * lax.axis_size("ch"))
    scale_factor = lax.rsqrt(total_squares / entries + 1e-06)
    return (query_grad, key_raw_grad, value_grad, lag_grad * scale_factor, short_grad)


def solution(mesh):
    in_specs = (
        P("ctx", "ch"),
        P("ctx", "ch"),
        P("ctx", "ch"),
        P("ctx", "ch"),
        P("ctx", "ch"),
        P("ctx", "ch"),
        P(None, "ch"),
    )
    out_specs = (P("ctx", "ch"), P("ctx", "ch"), P("ctx", "ch"), P("ctx", "ch"), P(None, "ch"))
    return jax.shard_map(
        per_device, mesh=mesh, in_specs=in_specs, out_specs=out_specs, check_vma=False
    )
```

profile of v0, /device:TPU:1, one launch (start us, length us, event | category | flops | bytes accessed | tf_op | source)
XLA Modules:
  0.0 756.4 jit_solution(221422856139085992)
XLA Ops:
  25.2 40.3 %all-gather.3.cloned.1.call-done = bf16[4096,1024]{1,0:T(8,128)(2,1)} async-done(((bf16[256,1024]{1,0:T(8,128)(2,1)}), bf16[4096,1024]{1,0:T(8,128)(2,1)}) %all-gather.3.cloned.1.call-update) | async-done | bytes 8388624 | tf_op jit(solution)/shard_map/all_gather | solution.py:56
  67.3 53.5 %all-gather.5.cloned.1.call-done = bf16[4096,1024]{1,0:T(8,128)(2,1)} async-done(((bf16[256,1024]{1,0:T(8,128)(2,1)}), bf16[4096,1024]{1,0:T(8,128)(2,1)}) %all-gather.5.cloned.1.call-update) | async-done | bytes 8388624 | tf_op jit(solution)/shard_map/all_gather | solution.py:57
  125.9 468.7 %while.23 = (s32[]{:T(128)}, f32[512,1024]{1,0:T(8,128)}, f32[512,1024]{1,0:T(8,128)}, f32[512,1024]{1,0:T(8,128)}, f32[512,1024]{1,0:T(8,128)}, /*index=5*/bf16...) while((s32[]{:T(128)}, f32[512,1024]{1,0:T(8,128)}, ...), condition=%wide.region_1.2_spmd.clone.clone, body=%wide.region_0.1_spmd.clone.clone.sunk | while | flops 1639981824 | bytes 53486816 | solution.py:83
  132.1 12.8 %convolution_bitcast_fusion.2 = f32[512,3072]{1,0:T(8,128)S(1)} fusion(bf16[512,512]{1,0:T(8,128)(2,1)} %get-tuple-element.451, bf16[256,1024]{1,0:T(8,128)(2,1)} %copy.23, bf16[256,1024]{1,0:T(8,128)(2,1)S(1)} %constant_dynamic-slice_fusion.4, bf16[256,1024]{1,0:T(8,128)(2,1)S(1)} %constant_dynamic-slice_fusion.5), kind=kOutput, calls=%fused_computation.2.clone.1 | convolution fusion | flops 1629487104 | bytes 8388608 | tf_op jit(solution)/shard_map/while/body/eval_jaxpr/dot_general | solution.py:39
  162.1 12.8 %convolution_bitcast_fusion.2 = f32[512,3072]{1,0:T(8,128)S(1)} fusion(bf16[512,512]{1,0:T(8,128)(2,1)} %get-tuple-element.451, bf16[256,1024]{1,0:T(8,128)(2,1)} %copy.23, bf16[256,1024]{1,0:T(8,128)(2,1)S(1)} %constant_dynamic-slice_fusion.4, bf16[256,1024]{1,0:T(8,128)(2,1)S(1)} %constant_dynamic-slice_fusion.5), kind=kOutput, calls=%fused_computation.2.clone.1 | convolution fusion | flops 1629487104 | bytes 8388608 | tf_op jit(solution)/shard_map/while/body/eval_jaxpr/dot_general | solution.py:39
  181.9 5.6 maximum_add_fusion.5
  193.5 12.8 %convolution_bitcast_fusion.2 = f32[512,3072]{1,0:T(8,128)S(1)} fusion(bf16[512,512]{1,0:T(8,128)(2,1)} %get-tuple-element.451, bf16[256,1024]{1,0:T(8,128)(2,1)} %copy.23, bf16[256,1024]{1,0:T(8,128)(2,1)S(1)} %constant_dynamic-slice_fusion.4, bf16[256,1024]{1,0:T(8,128)(2,1)S(1)} %constant_dynamic-slice_fusion.5), kind=kOutput, calls=%fused_computation.2.clone.1 | convolution fusion | flops 1629487104 | bytes 8388608 | tf_op jit(solution)/shard_map/while/body/eval_jaxpr/dot_general | solution.py:39
  213.2 5.6 maximum_add_fusion.5
  224.8 12.8 %convolution_bitcast_fusion.2 = f32[512,3072]{1,0:T(8,128)S(1)} fusion(bf16[512,512]{1,0:T(8,128)(2,1)} %get-tuple-element.451, bf16[256,1024]{1,0:T(8,128)(2,1)} %copy.23, bf16[256,1024]{1,0:T(8,128)(2,1)S(1)} %constant_dynamic-slice_fusion.4, bf16[256,1024]{1,0:T(8,128)(2,1)S(1)} %constant_dynamic-slice_fusion.5), kind=kOutput, calls=%fused_computation.2.clone.1 | convolution fusion | flops 1629487104 | bytes 8388608 | tf_op jit(solution)/shard_map/while/body/eval_jaxpr/dot_general | solution.py:39
  244.5 5.6 maximum_add_fusion.5
  256.1 12.8 %convolution_bitcast_fusion.2 = f32[512,3072]{1,0:T(8,128)S(1)} fusion(bf16[512,512]{1,0:T(8,128)(2,1)} %get-tuple-element.451, bf16[256,1024]{1,0:T(8,128)(2,1)} %copy.23, bf16[256,1024]{1,0:T(8,128)(2,1)S(1)} %constant_dynamic-slice_fusion.4, bf16[256,1024]{1,0:T(8,128)(2,1)S(1)} %constant_dynamic-slice_fusion.5), kind=kOutput, calls=%fused_computation.2.clone.1 | convolution fusion | flops 1629487104 | bytes 8388608 | tf_op jit(solution)/shard_map/while/body/eval_jaxpr/dot_general | solution.py:39
  275.9 5.6 maximum_add_fusion.5
  287.4 12.8 %convolution_bitcast_fusion.2 = f32[512,3072]{1,0:T(8,128)S(1)} fusion(bf16[512,512]{1,0:T(8,128)(2,1)} %get-tuple-element.451, bf16[256,1024]{1,0:T(8,128)(2,1)} %copy.23, bf16[256,1024]{1,0:T(8,128)(2,1)S(1)} %constant_dynamic-slice_fusion.4, bf16[256,1024]{1,0:T(8,128)(2,1)S(1)} %constant_dynamic-slice_fusion.5), kind=kOutput, calls=%fused_computation.2.clone.1 | convolution fusion | flops 1629487104 | bytes 8388608 | tf_op jit(solution)/shard_map/while/body/eval_jaxpr/dot_general | solution.py:39
  307.2 5.6 maximum_add_fusion.5
  318.7 12.8 %convolution_bitcast_fusion.2 = f32[512,3072]{1,0:T(8,128)S(1)} fusion(bf16[512,512]{1,0:T(8,128)(2,1)} %get-tuple-element.451, bf16[256,1024]{1,0:T(8,128)(2,1)} %copy.23, bf16[256,1024]{1,0:T(8,128)(2,1)S(1)} %constant_dynamic-slice_fusion.4, bf16[256,1024]{1,0:T(8,128)(2,1)S(1)} %constant_dynamic-slice_fusion.5), kind=kOutput, calls=%fused_computation.2.clone.1 | convolution fusion | flops 1629487104 | bytes 8388608 | tf_op jit(solution)/shard_map/while/body/eval_jaxpr/dot_general | solution.py:39
  338.5 5.6 maximum_add_fusion.5
  350.1 12.8 %convolution_bitcast_fusion.2 = f32[512,3072]{1,0:T(8,128)S(1)} fusion(bf16[512,512]{1,0:T(8,128)(2,1)} %get-tuple-element.451, bf16[256,1024]{1,0:T(8,128)(2,1)} %copy.23, bf16[256,1024]{1,0:T(8,128)(2,1)S(1)} %constant_dynamic-slice_fusion.4, bf16[256,1024]{1,0:T(8,128)(2,1)S(1)} %constant_dynamic-slice_fusion.5), kind=kOutput, calls=%fused_computation.2.clone.1 | convolution fusion | flops 1629487104 | bytes 8388608 | tf_op jit(solution)/shard_map/while/body/eval_jaxpr/dot_general | solution.py:39
  369.8 5.6 maximum_add_fusion.5
  381.4 12.8 %convolution_bitcast_fusion.2 = f32[512,3072]{1,0:T(8,128)S(1)} fusion(bf16[512,512]{1,0:T(8,128)(2,1)} %get-tuple-element.451, bf16[256,1024]{1,0:T(8,128)(2,1)} %copy.23, bf16[256,1024]{1,0:T(8,128)(2,1)S(1)} %constant_dynamic-slice_fusion.4, bf16[256,1024]{1,0:T(8,128)(2,1)S(1)} %constant_dynamic-slice_fusion.5), kind=kOutput, calls=%fused_computation.2.clone.1 | convolution fusion | flops 1629487104 | bytes 8388608 | tf_op jit(solution)/shard_map/while/body/eval_jaxpr/dot_general | solution.py:39
  401.1 5.6 maximum_add_fusion.5
  412.7 12.8 %convolution_bitcast_fusion.2 = f32[512,3072]{1,0:T(8,128)S(1)} fusion(bf16[512,512]{1,0:T(8,128)(2,1)} %get-tuple-element.451, bf16[256,1024]{1,0:T(8,128)(2,1)} %copy.23, bf16[256,1024]{1,0:T(8,128)(2,1)S(1)} %constant_dynamic-slice_fusion.4, bf16[256,1024]{1,0:T(8,128)(2,1)S(1)} %constant_dynamic-slice_fusion.5), kind=kOutput, calls=%fused_computation.2.clone.1 | convolution fusion | flops 1629487104 | bytes 8388608 | tf_op jit(solution)/shard_map/while/body/eval_jaxpr/dot_general | solution.py:39
  432.5 5.6 maximum_add_fusion.5
  444.0 12.8 %convolution_bitcast_fusion.2 = f32[512,3072]{1,0:T(8,128)S(1)} fusion(bf16[512,512]{1,0:T(8,128)(2,1)} %get-tuple-element.451, bf16[256,1024]{1,0:T(8,128)(2,1)} %copy.23, bf16[256,1024]{1,0:T(8,128)(2,1)S(1)} %constant_dynamic-slice_fusion.4, bf16[256,1024]{1,0:T(8,128)(2,1)S(1)} %constant_dynamic-slice_fusion.5), kind=kOutput, calls=%fused_computation.2.clone.1 | convolution fusion | flops 1629487104 | bytes 8388608 | tf_op jit(solution)/shard_map/while/body/eval_jaxpr/dot_general | solution.py:39
  475.3 12.8 %convolution_bitcast_fusion.2 = f32[512,3072]{1,0:T(8,128)S(1)} fusion(bf16[512,512]{1,0:T(8,128)(2,1)} %get-tuple-element.451, bf16[256,1024]{1,0:T(8,128)(2,1)} %copy.23, bf16[256,1024]{1,0:T(8,128)(2,1)S(1)} %constant_dynamic-slice_fusion.4, bf16[256,1024]{1,0:T(8,128)(2,1)S(1)} %constant_dynamic-slice_fusion.5), kind=kOutput, calls=%fused_computation.2.clone.1 | convolution fusion | flops 1629487104 | bytes 8388608 | tf_op jit(solution)/shard_map/while/body/eval_jaxpr/dot_general | solution.py:39
  506.6 12.8 %convolution_bitcast_fusion.2 = f32[512,3072]{1,0:T(8,128)S(1)} fusion(bf16[512,512]{1,0:T(8,128)(2,1)} %get-tuple-element.451, bf16[256,1024]{1,0:T(8,128)(2,1)} %copy.23, bf16[256,1024]{1,0:T(8,128)(2,1)S(1)} %constant_dynamic-slice_fusion.4, bf16[256,1024]{1,0:T(8,128)(2,1)S(1)} %constant_dynamic-slice_fusion.5), kind=kOutput, calls=%fused_computation.2.clone.1 | convolution fusion | flops 1629487104 | bytes 8388608 | tf_op jit(solution)/shard_map/while/body/eval_jaxpr/dot_general | solution.py:39
  526.4 5.6 maximum_add_fusion.5
  538.0 12.8 %convolution_bitcast_fusion.2 = f32[512,3072]{1,0:T(8,128)S(1)} fusion(bf16[512,512]{1,0:T(8,128)(2,1)} %get-tuple-element.451, bf16[256,1024]{1,0:T(8,128)(2,1)} %copy.23, bf16[256,1024]{1,0:T(8,128)(2,1)S(1)} %constant_dynamic-slice_fusion.4, bf16[256,1024]{1,0:T(8,128)(2,1)S(1)} %constant_dynamic-slice_fusion.5), kind=kOutput, calls=%fused_computation.2.clone.1 | convolution fusion | flops 1629487104 | bytes 8388608 | tf_op jit(solution)/shard_map/while/body/eval_jaxpr/dot_general | solution.py:39
  569.3 12.8 %convolution_bitcast_fusion.2 = f32[512,3072]{1,0:T(8,128)S(1)} fusion(bf16[512,512]{1,0:T(8,128)(2,1)} %get-tuple-element.451, bf16[256,1024]{1,0:T(8,128)(2,1)} %copy.23, bf16[256,1024]{1,0:T(8,128)(2,1)S(1)} %constant_dynamic-slice_fusion.4, bf16[256,1024]{1,0:T(8,128)(2,1)S(1)} %constant_dynamic-slice_fusion.5), kind=kOutput, calls=%fused_computation.2.clone.1 | convolution fusion | flops 1629487104 | bytes 8388608 | tf_op jit(solution)/shard_map/while/body/eval_jaxpr/dot_general | solution.py:39
  594.6 6.4 fusion.21
  607.3 5.8 fusion.17
  613.9 75.0 %psum.14 = f32[]{:T(128)} all-reduce(f32[]{:T(128)} %multiply_reduce_fusion.3), channel_id=1, replica_groups=mesh['ctx'=16,'ch'=8] {'ctx','ch'}, use_global_device_ids=true, to_apply=%region_3.4 | all-reduce | flops 1 | bytes 8 | tf_op jit(solution)/shard_map/psum | solution.py:137
  696.4 49.9 %psum.15 = f32[3,1024]{1,0:T(4,128)} all-reduce(f32[3,1024]{1,0:T(4,128)S(1)} %pad_maximum_fusion.2), channel_id=1, replica_groups=mesh['ctx'=16,'ch'=8] {'ctx'}, use_global_device_ids=true, to_apply=%region_7.8 | all-reduce | flops 3072 | bytes 24576 | tf_op jit(solution)/shard_map/psum | solution.py:135
  (211 shorter events, 262.5 us)
Async XLA Ops:
  7.2 8.2 %copy-start.5 = (bf16[256,1024]{1,0:T(8,128)(2,1)S(1)}, bf16[256,1024]{1,0:T(8,128)(2,1)}, u32[]{:S(2)}) copy-start(bf16[256,1024]{1,0:T(8,128)(2,1)} %param.11) | copy-start | bytes 1572868
  7.2 58.3 %all-gather.3.cloned.1.call-start = ((), (), s32[]{:S(2)}) async-start(), calls=%async_computation | async-start | bytes 8912896 | tf_op jit(solution)/shard_map/all_gather | solution.py:56
  7.9 112.9 %all-gather.5.cloned.1.call-start = ((), (), s32[]{:S(2)}) async-start(), calls=%async_computation.1 | async-start | bytes 8912896 | tf_op jit(solution)/shard_map/all_gather | solution.py:57
  8.7 5.4 collective-permute-start.1
  15.3 1.6 copy-start.2
  16.9 7.0 copy-start.7
  16.9 7.0 copy-start.8
  16.9 7.0 copy-start.9
  22.3 0.7 copy-start.6
  127.8 28.4 %collective-permute-start = (bf16[256,1024]{1,0:T(8,128)(2,1)}, bf16[256,1024]{1,0:T(8,128)(2,1)}, u32[]{:S(2)}, u32[]{:S(2)}) collective-permute-start(bf16[256,1024]{1,0:T(8,128)(2,1)} %copy.23), channel_id=1, source_target_pairs={{8,0},{16,8},{24,16},{32,24},{40,32},{48,40},{56,48},{64,56},{72,6... | collective-permute-start | bytes 1572872 | tf_op jit(solution)/shard_map/while/body/eval_jaxpr/ppermute | solution.py:14
  158.0 29.5 %collective-permute-start = (bf16[256,1024]{1,0:T(8,128)(2,1)}, bf16[256,1024]{1,0:T(8,128)(2,1)}, u32[]{:S(2)}, u32[]{:S(2)}) collective-permute-start(bf16[256,1024]{1,0:T(8,128)(2,1)} %copy.23), channel_id=1, source_target_pairs={{8,0},{16,8},{24,16},{32,24},{40,32},{48,40},{56,48},{64,56},{72,6... | collective-permute-start | bytes 1572872 | tf_op jit(solution)/shard_map/while/body/eval_jaxpr/ppermute | solution.py:14
  189.3 29.4 %collective-permute-start = (bf16[256,1024]{1,0:T(8,128)(2,1)}, bf16[256,1024]{1,0:T(8,128)(2,1)}, u32[]{:S(2)}, u32[]{:S(2)}) collective-permute-start(bf16[256,1024]{1,0:T(8,128)(2,1)} %copy.23), channel_id=1, source_target_pairs={{8,0},{16,8},{24,16},{32,24},{40,32},{48,40},{56,48},{64,56},{72,6... | collective-permute-start | bytes 1572872 | tf_op jit(solution)/shard_map/while/body/eval_jaxpr/ppermute | solution.py:14
  220.7 29.4 %collective-permute-start = (bf16[256,1024]{1,0:T(8,128)(2,1)}, bf16[256,1024]{1,0:T(8,128)(2,1)}, u32[]{:S(2)}, u32[]{:S(2)}) collective-permute-start(bf16[256,1024]{1,0:T(8,128)(2,1)} %copy.23), channel_id=1, source_target_pairs={{8,0},{16,8},{24,16},{32,24},{40,32},{48,40},{56,48},{64,56},{72,6... | collective-permute-start | bytes 1572872 | tf_op jit(solution)/shard_map/while/body/eval_jaxpr/ppermute | solution.py:14
  252.0 29.4 %collective-permute-start = (bf16[256,1024]{1,0:T(8,128)(2,1)}, bf16[256,1024]{1,0:T(8,128)(2,1)}, u32[]{:S(2)}, u32[]{:S(2)}) collective-permute-start(bf16[256,1024]{1,0:T(8,128)(2,1)} %copy.23), channel_id=1, source_target_pairs={{8,0},{16,8},{24,16},{32,24},{40,32},{48,40},{56,48},{64,56},{72,6... | collective-permute-start | bytes 1572872 | tf_op jit(solution)/shard_map/while/body/eval_jaxpr/ppermute | solution.py:14
  283.3 29.4 %collective-permute-start = (bf16[256,1024]{1,0:T(8,128)(2,1)}, bf16[256,1024]{1,0:T(8,128)(2,1)}, u32[]{:S(2)}, u32[]{:S(2)}) collective-permute-start(bf16[256,1024]{1,0:T(8,128)(2,1)} %copy.23), channel_id=1, source_target_pairs={{8,0},{16,8},{24,16},{32,24},{40,32},{48,40},{56,48},{64,56},{72,6... | collective-permute-start | bytes 1572872 | tf_op jit(solution)/shard_map/while/body/eval_jaxpr/ppermute | solution.py:14
  314.6 29.4 %collective-permute-start = (bf16[256,1024]{1,0:T(8,128)(2,1)}, bf16[256,1024]{1,0:T(8,128)(2,1)}, u32[]{:S(2)}, u32[]{:S(2)}) collective-permute-start(bf16[256,1024]{1,0:T(8,128)(2,1)} %copy.23), channel_id=1, source_target_pairs={{8,0},{16,8},{24,16},{32,24},{40,32},{48,40},{56,48},{64,56},{72,6... | collective-permute-start | bytes 1572872 | tf_op jit(solution)/shard_map/while/body/eval_jaxpr/ppermute | solution.py:14
  345.9 29.4 %collective-permute-start = (bf16[256,1024]{1,0:T(8,128)(2,1)}, bf16[256,1024]{1,0:T(8,128)(2,1)}, u32[]{:S(2)}, u32[]{:S(2)}) collective-permute-start(bf16[256,1024]{1,0:T(8,128)(2,1)} %copy.23), channel_id=1, source_target_pairs={{8,0},{16,8},{24,16},{32,24},{40,32},{48,40},{56,48},{64,56},{72,6... | collective-permute-start | bytes 1572872 | tf_op jit(solution)/shard_map/while/body/eval_jaxpr/ppermute | solution.py:14
  377.2 29.4 %collective-permute-start = (bf16[256,1024]{1,0:T(8,128)(2,1)}, bf16[256,1024]{1,0:T(8,128)(2,1)}, u32[]{:S(2)}, u32[]{:S(2)}) collective-permute-start(bf16[256,1024]{1,0:T(8,128)(2,1)} %copy.23), channel_id=1, source_target_pairs={{8,0},{16,8},{24,16},{32,24},{40,32},{48,40},{56,48},{64,56},{72,6... | collective-permute-start | bytes 1572872 | tf_op jit(solution)/shard_map/while/body/eval_jaxpr/ppermute | solution.py:14
  408.6 29.4 %collective-permute-start = (bf16[256,1024]{1,0:T(8,128)(2,1)}, bf16[256,1024]{1,0:T(8,128)(2,1)}, u32[]{:S(2)}, u32[]{:S(2)}) collective-permute-start(bf16[256,1024]{1,0:T(8,128)(2,1)} %copy.23), channel_id=1, source_target_pairs={{8,0},{16,8},{24,16},{32,24},{40,32},{48,40},{56,48},{64,56},{72,6... | collective-permute-start | bytes 1572872 | tf_op jit(solution)/shard_map/while/body/eval_jaxpr/ppermute | solution.py:14
  439.9 29.4 %collective-permute-start = (bf16[256,1024]{1,0:T(8,128)(2,1)}, bf16[256,1024]{1,0:T(8,128)(2,1)}, u32[]{:S(2)}, u32[]{:S(2)}) collective-permute-start(bf16[256,1024]{1,0:T(8,128)(2,1)} %copy.23), channel_id=1, source_target_pairs={{8,0},{16,8},{24,16},{32,24},{40,32},{48,40},{56,48},{64,56},{72,6... | collective-permute-start | bytes 1572872 | tf_op jit(solution)/shard_map/while/body/eval_jaxpr/ppermute | solution.py:14
  471.2 29.4 %collective-permute-start = (bf16[256,1024]{1,0:T(8,128)(2,1)}, bf16[256,1024]{1,0:T(8,128)(2,1)}, u32[]{:S(2)}, u32[]{:S(2)}) collective-permute-start(bf16[256,1024]{1,0:T(8,128)(2,1)} %copy.23), channel_id=1, source_target_pairs={{8,0},{16,8},{24,16},{32,24},{40,32},{48,40},{56,48},{64,56},{72,6... | collective-permute-start | bytes 1572872 | tf_op jit(solution)/shard_map/while/body/eval_jaxpr/ppermute | solution.py:14
  502.5 29.4 %collective-permute-start = (bf16[256,1024]{1,0:T(8,128)(2,1)}, bf16[256,1024]{1,0:T(8,128)(2,1)}, u32[]{:S(2)}, u32[]{:S(2)}) collective-permute-start(bf16[256,1024]{1,0:T(8,128)(2,1)} %copy.23), channel_id=1, source_target_pairs={{8,0},{16,8},{24,16},{32,24},{40,32},{48,40},{56,48},{64,56},{72,6... | collective-permute-start | bytes 1572872 | tf_op jit(solution)/shard_map/while/body/eval_jaxpr/ppermute | solution.py:14
  533.8 29.4 %collective-permute-start = (bf16[256,1024]{1,0:T(8,128)(2,1)}, bf16[256,1024]{1,0:T(8,128)(2,1)}, u32[]{:S(2)}, u32[]{:S(2)}) collective-permute-start(bf16[256,1024]{1,0:T(8,128)(2,1)} %copy.23), channel_id=1, source_target_pairs={{8,0},{16,8},{24,16},{32,24},{40,32},{48,40},{56,48},{64,56},{72,6... | collective-permute-start | bytes 1572872 | tf_op jit(solution)/shard_map/while/body/eval_jaxpr/ppermute | solution.py:14
  565.1 29.4 %collective-permute-start = (bf16[256,1024]{1,0:T(8,128)(2,1)}, bf16[256,1024]{1,0:T(8,128)(2,1)}, u32[]{:S(2)}, u32[]{:S(2)}) collective-permute-start(bf16[256,1024]{1,0:T(8,128)(2,1)} %copy.23), channel_id=1, source_target_pairs={{8,0},{16,8},{24,16},{32,24},{40,32},{48,40},{56,48},{64,56},{72,6... | collective-permute-start | bytes 1572872 | tf_op jit(solution)/shard_map/while/body/eval_jaxpr/ppermute | solution.py:14
  603.7 1.6 copy-start
  603.7 2.2 copy-start.1
  607.3 82.3 %copy-start.3 = (f32[258,1024]{1,0:T(8,128)S(1)}, f32[258,1024]{1,0:T(8,128)}, u32[]{:S(2)}) copy-start(f32[258,1024]{1,0:T(8,128)} %copy-done.2) | copy-start | bytes 3170308
  692.7 1.0 copy-start.4
  693.6 52.7 %collective-permute-start.2 = (f32[2,1024]{1,0:T(2,128)S(1)}, f32[2,1024]{1,0:T(2,128)S(1)}, u32[]{:S(2)}, u32[]{:S(2)}) collective-permute-start(f32[2,1024]{1,0:T(2,128)S(1)} %slice.190), channel_id=1, source_target_pairs={{8,0},{16,8},{24,16},{32,24},{40,32},{48,40},{56,48},{64,56},{72,6... | collective-permute-start | bytes 24584 | tf_op jit(solution)/shard_map/ppermute | solution.py:14
Sparse Core Ops, SparseCore 0:
  9.7 55.7 all-gather.2
  67.7 53.0 all-gather.4
where the time goes:
time: 763 us; the launch traced here: 756 us
  other arithmetic  209 us (27%)
  matrix products  204 us (27%)
  blocking collectives  125 us (16%)
  waiting for transfers between devices  94.6 us (12%)
  local copies, waits for them, and re-layouts  71.7 us (9%)
  starting transfers between devices  36.3 us (5%)
  between operations  15 us (2%)
    dot_general x16, matrix products, forward(): return jnp.dot(forward_pair, doubled, preferred_element_type=jnp.float32)  198 us
    add x16, other arithmetic, pair_step(): out_acc + conj_product(filter_spec + parity * prev_filter, grad_spec, dc_...  83.3 us
    add x15, other arithmetic, pair_step(): gated_spec + parity * prev_gated  75.7 us
    psum x1, blocking collectives, per_device(): total_squares = lax.psum(squares, ('ctx', 'ch'))  75 us
    all_gather x1, waiting for transfers between devices, sequence_blocks(): gateds = lax.all_gather(gated, 'ctx', axis=0, tiled=True)  53.5 us
    psum x1, blocking collectives, per_device(): short_grad = lax.psum(tap_terms, 'ctx')  49.9 us
    all_gather x1, waiting for transfers between devices, sequence_blocks(): filters = lax.all_gather(long_filter, 'ctx', axis=0, tiled=True)  40.3 us
    ppermute x17, starting transfers between devices, shifted(): return lax.ppermute(block, axis, route)  36.2 us
  transfers between devices with their start and end apart: 19, of which 2 were waited for; matrix products, arithmetic and copies ran while one was open for 56% of the time, Pallas kernels for 0%

commit v1 on v0

v1 whole, which is shorter than its diff:
```python
import functools

import jax
import jax.numpy as jnp
import ml_dtypes
import numpy as np
from jax import lax
from jax.experimental import pallas as pl
from jax.experimental.pallas import tpu as pltpu
from jax.sharding import PartitionSpec as P

MESH = pl.DeviceIdType.MESH
F32, BF16 = jnp.float32, jnp.bfloat16
ROWS, WIDTH, LANES, CHIPS, BLOCKS = 256, 1024, 128, 8, 16
TAPS = 3
STEPS = ((0, 1), (1, 0), (0, 3), (1, 1), (0, 2), (1, 3), (1, 2))


def tables():
    length = 2 * ROWS
    rows = np.arange(length)
    freq = np.where(rows <= ROWS, rows, rows - ROWS)
    angle = (freq[:, None] * np.arange(ROWS)[None, :] % length) * (np.pi / ROWS)
    forward = np.where((rows <= ROWS)[:, None], np.cos(angle), -np.sin(angle))
    weight = np.where((freq == 0) | (freq == ROWS), 1.0, 2.0) / length
    inverse = forward.T * weight[None, :]

    def pair(table):
        upper = table.astype(ml_dtypes.bfloat16)
        lower = (table - upper.astype(np.float64)).astype(ml_dtypes.bfloat16)
        return np.concatenate([upper, lower], axis=0)

    return pair(forward), pair(inverse)


def lanes(index):
    return pl.ds(pl.multiple_of(index * LANES, LANES), LANES)


def kernel(
    qb_hbm, kr_hbm, vb_hbm, co_hbm, og_hbm, lf_hbm, taps_ref, fwd_hbm, inv_hbm,
    qg_hbm, krg_hbm, vg_hbm, fg_hbm, sg_ref,
    qb, kr, vb, co, og, lf, fwd, inv,
    cg, gated, ext, conv, halo, land_g, land_a, spec_g, sum_g, spec_a, dif_a,
    prod_hi, prod_lo, back, ret, keyg, tail, qg, krg, vg, fg,
    part, part_land, short, squares, squares_land, total, total_land,
    in_sem, out_sem, halo_sem, tail_sem,
    gs_sem, gr_sem, fs_sem, fr_sem, as_sem, ar_sem, own_sem, rs_sem, rr_sem,
    ps_sem, pr_sem, bs_sem, br_sem, s1s_sem, s1r_sem, s2s_sem, s2r_sem,
):
    me = lax.axis_index("ctx")
    group = lax.axis_index("ch")
    chip, core = me // 2, lax.rem(me, 2)
    sibling = chip * 2 + 1 - core
    chip_x, chip_y = chip // 4, lax.rem(chip, 4)

    def chip_at(dx, dy):
        return lax.rem(chip_x + dx, 2) * 4 + lax.rem(chip_y + dy, 4)

    dests = [chip_at(dx, dy) for dx, dy in STEPS]
    sources = [chip_at(2 - dx, 4 - dy) for dx, dy in STEPS]

    def remote(src, dst, send, recv, ctx):
        return pltpu.make_async_remote_copy(
            src_ref=src, dst_ref=dst, send_sem=send, recv_sem=recv,
            device_id={"ctx": ctx}, device_id_type=MESH,
        )

    def arrived(ref, sem):
        pltpu.make_async_copy(ref, ref, sem).wait()

    loads = [
        pltpu.make_async_copy(src, dst, in_sem.at[n])
        for n, (src, dst) in enumerate(
            ((og_hbm, og), (qb_hbm, qb), (kr_hbm, kr), (lf_hbm, lf), (vb_hbm, vb),
             (fwd_hbm, fwd), (co_hbm, co), (inv_hbm, inv))
        )
    ]
    for load in loads:
        load.start()
    og_in, qb_in, kr_in, lf_in, vb_in, fwd_in, co_in, inv_in = loads

    barrier = pltpu.get_barrier_semaphore()
    for step in range(1, BLOCKS):
        pl.semaphore_signal(
            barrier, inc=1, device_id={"ctx": lax.rem(me + step, BLOCKS)}, device_id_type=MESH
        )
    for step in range(1, 8):
        pl.semaphore_signal(
            barrier, inc=1, device_id={"ch": lax.rem(group + step, 8)}, device_id_type=MESH
        )

    og_in.wait()
    qb_in.wait()

    def make_grad(p, carry):
        at = lanes(p)
        cg[:, at] = (og[:, at].astype(F32) * qb[:, at].astype(F32)).astype(BF16)
        return carry

    lax.fori_loop(0, CHIPS, make_grad, 0)
    kr_in.wait()
    lf_in.wait()
    pl.semaphore_wait(barrier, BLOCKS - 1 + 7)

    def halo_copy():
        return remote(
            kr.at[pl.ds(ROWS - 16, 16)], halo, halo_sem.at[0], halo_sem.at[1],
            lax.rem(me + 1, BLOCKS),
        )

    @pl.when(me < BLOCKS - 1)
    def _():
        halo_copy().start()

    mine = lanes(core)
    own_grad = remote(
        cg.at[:, lanes(chip)], land_g.at[chip, :, mine], gs_sem.at[7], fr_sem.at[chip], sibling
    )
    own_grad.start()
    grad_sends = [own_grad]
    for n, p in enumerate(dests):
        copy = remote(
            cg.at[:, lanes(p)], land_g.at[chip, :, mine], gs_sem.at[n], gr_sem.at[chip],
            p * 2 + core,
        )
        copy.start()
        grad_sends.append(copy)
    keep_grad = pltpu.make_async_copy(
        cg.at[:, lanes(chip)], land_g.at[chip, :, mine], own_sem.at[0]
    )
    keep_grad.start()

    def send_to_core(block, goal, first):
        copies = []
        for n, p in enumerate(dests):
            copy = remote(
                block.at[:, lanes(p)], land_a.at[chip, :, mine], as_sem.at[first + n],
                ar_sem.at[me], p * 2 + goal,
            )
            copy.start()
            copies.append(copy)

        @pl.when(core == goal)
        def _():
            pltpu.make_async_copy(
                block.at[:, lanes(chip)], land_a.at[chip, :, mine], own_sem.at[1]
            ).start()

        @pl.when(core != goal)
        def _():
            remote(
                block.at[:, lanes(chip)], land_a.at[chip, :, mine], as_sem.at[first + 7],
                ar_sem.at[me], sibling,
            ).start()

        return copies

    filter_sends = send_to_core(lf, 0, 0)

    vb_in.wait()

    @pl.when(me > 0)
    def _():
        arrived(halo, halo_sem.at[1])
        ext[0:8, :] = halo[...].astype(F32)[8:16]

    @pl.when(me == 0)
    def _():
        ext[0:8, :] = jnp.zeros((8, WIDTH), F32)

    def make_gated(p, carry):
        at = lanes(p)
        ext[8:, at] = kr[:, at].astype(F32)
        value = jnp.zeros((ROWS, LANES), F32)
        for j in range(TAPS):
            value = value + taps_ref[j : j + 1, at] * ext[8 - j : 8 - j + ROWS, at]
        conv[:, at] = value
        gated[:, at] = (value * vb[:, at].astype(F32)).astype(BF16)
        return carry

    lax.fori_loop(0, CHIPS, make_gated, 0)
    gated_sends = send_to_core(gated, 1, 8)

    co_in.wait()

    def make_query(p, carry):
        at = lanes(p)
        qg[:, at] = (og[:, at].astype(F32) * co[:, at].astype(F32)).astype(BF16)
        return carry

    lax.fori_loop(0, CHIPS, make_query, 0)
    qg_out = pltpu.make_async_copy(qg, qg_hbm, out_sem.at[0])
    qg_out.start()

    fwd_in.wait()

    def transform(block):
        upper = jnp.dot(fwd[: 2 * ROWS], block, preferred_element_type=F32)
        return upper + jnp.dot(fwd[2 * ROWS :], block, preferred_element_type=F32)

    other = lanes(1 - core)

    def grad_spectrum(source):
        arrived(land_g.at[source, :, other], fr_sem.at[source])
        spec_g[source] = transform(land_g[source])

    spec_g[CHIPS] = jnp.zeros((2 * ROWS, 2 * LANES), F32)
    keep_grad.wait()
    waiting = chip
    forwards = []
    for n, source in enumerate(sources):
        block = land_g.at[source, :, mine]
        arrived(block, gr_sem.at[source])
        copy = remote(block, block, fs_sem.at[n], fr_sem.at[source], sibling)
        copy.start()
        forwards.append(copy)
        grad_spectrum(waiting)
        waiting = source
    grad_spectrum(waiting)

    def join(m, carry):
        even = (lax.broadcasted_iota(jnp.int32, (2 * ROWS, LANES), 0) % 2) == 0
        first, second = spec_g[m, :, :LANES], spec_g[m, :, LANES:]
        third = spec_g[m + 1, :, :LANES]
        first = first + jnp.where(even, second, -second)
        second = second + jnp.where(even, third, -third)
        spec_g[m, :, :LANES] = first
        spec_g[m, :, LANES:] = second
        sum_g[m, :, :LANES] = first[:ROWS] + first[ROWS:]
        sum_g[m, :, LANES:] = second[:ROWS] + second[ROWS:]
        return carry

    lax.fori_loop(0, CHIPS, join, 0)

    def a_spectrum(source):
        result = transform(land_a[source])
        spec_a[source] = result
        dif_a[source] = result[:ROWS] - result[ROWS:]

    arrived(land_a.at[chip, :, mine], own_sem.at[1])
    arrived(land_a.at[chip, :, other], ar_sem.at[sibling])
    a_spectrum(chip)
    for source in sources:
        arrived(land_a.at[source, :, :LANES], ar_sem.at[source * 2])
        arrived(land_a.at[source, :, LANES:], ar_sem.at[source * 2 + 1])
        a_spectrum(source)

    def products(chunk, carry):
        for base in range(0, BLOCKS, 4):
            halves = []
            for sub in range(2):
                row = pl.multiple_of(chunk * 16 + sub * 8, 8)
                re_at, im_at = pl.ds(row, 8), pl.ds(pl.multiple_of(row + ROWS, 8), 8)
                real = [None] * 4
                both = [None] * 4
                cross = [None] * 4
                held = []
                for m in range(base, BLOCKS):
                    at = slice((m % 2) * LANES, (m % 2 + 1) * LANES)
                    g_re, g_im = spec_g[m // 2, re_at, at], spec_g[m // 2, im_at, at]
                    g_sum = sum_g[m // 2, re_at, at]
                    j = m - base
                    at = slice((j % 2) * LANES, (j % 2 + 1) * LANES)
                    held.append(
                        (spec_a[j // 2, re_at, at], spec_a[j // 2, im_at, at], dif_a[j // 2, re_at, at])
                    )
                    for u in range(min(4, j + 1)):
                        a_re, a_im, a_dif = held[j - u]
                        terms = (a_re * g_re, a_im * g_im, a_dif * g_sum)
                        for sums, term in zip((real, both, cross), terms):
                            sums[u] = term if sums[u] is None else sums[u] + term
                edge = (lax.broadcasted_iota(jnp.int32, (8, LANES), 0) + row) == 0
                halves.append(
                    [
                        (
                            jnp.where(edge, real[u], real[u] + both[u]),
                            jnp.where(edge, both[u], cross[u] - real[u] + both[u]),
                        )
                        for u in range(4)
                    ]
                )
            start = pl.multiple_of(chunk * 16, 16)
            for u in range(4):
                at = slice((base + u) * LANES, (base + u + 1) * LANES)
                for part_at, offset in ((0, 0), (1, ROWS)):
                    value = jnp.concatenate([halves[0][u][part_at], halves[1][u][part_at]], axis=0)
                    upper = value.astype(BF16)
                    rows_at = pl.ds(pl.multiple_of(start + offset, 16), 16)
                    prod_hi[rows_at, at] = upper
                    prod_lo[rows_at, at] = (value - upper.astype(F32)).astype(BF16)
        return carry

    lax.fori_loop(0, ROWS // 16, products, 0)

    inv_in.wait()
    squares[...] = jnp.zeros((8, LANES), F32)

    def restore(p):
        at = pl.ds(pl.multiple_of(p * 2 * LANES, 2 * LANES), 2 * LANES)
        upper = prod_hi[:, at]
        both = jnp.dot(inv[...], upper, preferred_element_type=F32)
        result = both[:ROWS] + both[ROWS:]
        result = result + jnp.dot(inv[:ROWS], prod_lo[:, at], preferred_element_type=F32)
        back[p] = result.astype(BF16)
        square = result[:, :LANES] * result[:, :LANES] + result[:, LANES:] * result[:, LANES:]
        squares[...] += jnp.sum(square.reshape(ROWS // 8, 8, LANES), axis=0)

    returns = []

    def give_back(n, p, half):
        copy = remote(
            back.at[p, :, half * LANES : (half + 1) * LANES], ret.at[core, :, lanes(chip)],
            rs_sem.at[n * 2 + half], rr_sem.at[core * 8 + chip], p * 2 + half,
        )
        copy.start()
        returns.append(copy)

    for n, p in enumerate(dests):
        restore(p)
        give_back(n, p, 0)
        give_back(n, p, 1)
    restore(chip)
    keep_back = pltpu.make_async_copy(
        back.at[chip, :, mine], ret.at[core, :, lanes(chip)], own_sem.at[0]
    )
    keep_back.start()
    own_back = remote(
        back.at[chip, :, other], ret.at[core, :, lanes(chip)],
        rs_sem.at[14], rr_sem.at[core * 8 + chip], sibling,
    )
    own_back.start()

    def squares_copy(step):
        return remote(
            squares, squares_land.at[chip], s1s_sem.at[step], s1r_sem.at[chip],
            lax.rem(me + step, BLOCKS),
        )

    @pl.when(core == 1)
    def _():
        for step in range(1, BLOCKS):
            squares_copy(step).start()
        squares_land[chip] = squares[...]

    part[...] = jnp.zeros((8, WIDTH), F32)
    keep_back.wait()

    def branch(source):
        at = lanes(source)
        wide = ret[0, :, at].astype(F32)
        vg[:, at] = (wide * conv[:, at]).astype(BF16)
        key = wide * vb[:, at].astype(F32)
        keyg[0:ROWS, at] = key
        for j in range(TAPS):
            part[j : j + 1, at] = jnp.sum(key * ext[8 - j : 8 - j + ROWS, at], axis=0, keepdims=True)

    @pl.when(core == 1)
    def _():
        arrived(ret.at[0, :, lanes(chip)], rr_sem.at[chip])

    branch(chip)
    for source in sources:
        arrived(ret.at[0, :, lanes(source)], rr_sem.at[source])
        branch(source)
    vg_out = pltpu.make_async_copy(vg, vg_hbm, out_sem.at[1])
    vg_out.start()

    def tail_copy():
        return remote(
            keyg.at[pl.ds(0, 8)], tail, tail_sem.at[0], tail_sem.at[1],
            lax.rem(me + BLOCKS - 1, BLOCKS),
        )

    @pl.when(me > 0)
    def _():
        tail_copy().start()

    part_sends = []
    for n, p in enumerate(dests):
        copy = remote(
            part.at[:, lanes(p)], part_land.at[me], ps_sem.at[n], pr_sem.at[me], p * 2
        )
        copy.start()
        part_sends.append(copy)

    def part_copy():
        return remote(part.at[:, lanes(chip)], part_land.at[me], ps_sem.at[7], pr_sem.at[me], sibling)

    @pl.when(core == 1)
    def _():
        part_copy().start()

    @pl.when(core == 0)
    def _():
        part_land[me] = part[:, lanes(chip)]

    for source in sources:
        arrived(squares_land.at[source], s1r_sem.at[source])

    @pl.when(core == 0)
    def _():
        arrived(squares_land.at[chip], s1r_sem.at[chip])

    total[...] = jnp.sum(squares_land[...], axis=0)
    total_sends = []
    for step in range(1, 8):
        copy = pltpu.make_async_remote_copy(
            src_ref=total, dst_ref=total_land.at[group], send_sem=s2s_sem.at[step],
            recv_sem=s2r_sem.at[group], device_id={"ch": lax.rem(group + step, 8)},
            device_id_type=MESH,
        )
        copy.start()
        total_sends.append(copy)
    total_land[group] = total[...]

    @pl.when(me < BLOCKS - 1)
    def _():
        arrived(tail, tail_sem.at[1])
        keyg[ROWS : ROWS + 8, :] = tail[...]

    @pl.when(me == BLOCKS - 1)
    def _():
        keyg[ROWS : ROWS + 8, :] = jnp.zeros((8, WIDTH), F32)

    def make_raw(p, carry):
        at = lanes(p)
        value = jnp.zeros((ROWS, LANES), F32)
        for j in range(TAPS):
            value = value + taps_ref[j : j + 1, at] * keyg[j : j + ROWS, at]
        krg[:, at] = value.astype(BF16)
        return carry

    lax.fori_loop(0, CHIPS, make_raw, 0)
    krg_out = pltpu.make_async_copy(krg, krg_hbm, out_sem.at[2])
    krg_out.start()

    def short_copy(step):
        return remote(
            short.at[:, lanes(chip)], short.at[:, lanes(chip)], bs_sem.at[step], br_sem.at[chip],
            lax.rem(me + step, BLOCKS),
        )

    @pl.when(core == 0)
    def _():
        for source in sources:
            arrived(part_land.at[source * 2], pr_sem.at[source * 2])
            arrived(part_land.at[source * 2 + 1], pr_sem.at[source * 2 + 1])
        arrived(part_land.at[sibling], pr_sem.at[sibling])
        short[:, lanes(chip)] = jnp.sum(part_land[...], axis=0)
        for step in range(1, BLOCKS):
            short_copy(step).start()

    for step in range(1, 8):
        source = lax.rem(group + 8 - step, 8)
        arrived(total_land.at[source], s2r_sem.at[source])
    everything = jnp.sum(jnp.sum(total_land[...], axis=0), axis=(0, 1), keepdims=True)
    scale = lax.rsqrt(everything / float(4096 * 8192) + 1e-06)

    fg_outs = []

    def scaled(n, source):
        at = lanes(source)
        fg[:, at] = ret[1, :, at].astype(F32) * scale
        copy = pltpu.make_async_copy(fg.at[:, at], fg_hbm.at[:, at], out_sem.at[3 + n])
        copy.start()
        fg_outs.append(copy)

    @pl.when(core == 0)
    def _():
        arrived(ret.at[1, :, lanes(chip)], rr_sem.at[8 + chip])

    scaled(7, chip)
    for n, source in enumerate(sources):
        arrived(ret.at[1, :, lanes(source)], rr_sem.at[8 + source])
        scaled(n, source)

    for source in sources:
        arrived(short.at[:, lanes(source)], br_sem.at[source])

    @pl.when(core == 1)
    def _():
        arrived(short.at[:, lanes(chip)], br_sem.at[chip])

    sg_ref[...] = short[0:TAPS, :]

    for copy in grad_sends + filter_sends + gated_sends + forwards + returns + [own_back]:
        copy.wait_send()
    for copy in part_sends + total_sends:
        copy.wait_send()

    @pl.when(me < BLOCKS - 1)
    def _():
        halo_copy().wait_send()

    @pl.when(me > 0)
    def _():
        tail_copy().wait_send()

    @pl.when(core == 0)
    def _():
        for step in range(1, BLOCKS):
            short_copy(step).wait_send()
        remote(
            gated.at[:, lanes(chip)], land_a.at[chip, :, mine], as_sem.at[15], ar_sem.at[me], sibling
        ).wait_send()

    @pl.when(core == 1)
    def _():
        part_copy().wait_send()
        for step in range(1, BLOCKS):
            squares_copy(step).wait_send()
        remote(
            lf.at[:, lanes(chip)], land_a.at[chip, :, mine], as_sem.at[7], ar_sem.at[me], sibling
        ).wait_send()

    for copy in [qg_out, vg_out, krg_out] + fg_outs:
        copy.wait()


def per_device(query_branch, key_raw, value_branch, conv_out, out_grad, long_filter, short_filter):
    forward, inverse = tables()
    anywhere = pl.BlockSpec(memory_space=pl.ANY)
    in_vmem = pl.BlockSpec(memory_space=pltpu.VMEM)
    block = jax.ShapeDtypeStruct((ROWS, WIDTH), BF16)
    dma = pltpu.SemaphoreType.DMA
    vmem = pltpu.VMEM
    return pl.pallas_call(
        kernel,
        out_shape=(
            block, block, block,
            jax.ShapeDtypeStruct((ROWS, WIDTH), F32),
            jax.ShapeDtypeStruct((TAPS, WIDTH), F32),
        ),
        in_specs=[anywhere] * 6 + [in_vmem] + [anywhere] * 2,
        out_specs=(anywhere, anywhere, anywhere, anywhere, in_vmem),
        scratch_shapes=[
            *[vmem((ROWS, WIDTH), BF16)] * 6,
            vmem((4 * ROWS, ROWS), BF16),
            vmem((2 * ROWS, 2 * ROWS), BF16),
            vmem((ROWS, WIDTH), BF16),
            vmem((ROWS, WIDTH), BF16),
            vmem((ROWS + 8, WIDTH), F32),
            vmem((ROWS, WIDTH), F32),
            vmem((16, WIDTH), BF16),
            vmem((CHIPS, ROWS, 2 * LANES), BF16),
            vmem((CHIPS, ROWS, 2 * LANES), BF16),
            vmem((CHIPS + 1, 2 * ROWS, 2 * LANES), F32),
            vmem((CHIPS, ROWS, 2 * LANES), F32),
            vmem((CHIPS, 2 * ROWS, 2 * LANES), F32),
            vmem((CHIPS, ROWS, 2 * LANES), F32),
            vmem((2 * ROWS, BLOCKS * LANES), BF16),
            vmem((2 * ROWS, BLOCKS * LANES), BF16),
            vmem((CHIPS, ROWS, 2 * LANES), BF16),
            vmem((2, ROWS, WIDTH), BF16),
            vmem((ROWS + 8, WIDTH), F32),
            vmem((8, WIDTH), F32),
            *[vmem((ROWS, WIDTH), BF16)] * 3,
            vmem((ROWS, WIDTH), F32),
            vmem((8, WIDTH), F32),
            vmem((BLOCKS, 8, LANES), F32),
            vmem((8, WIDTH), F32),
            vmem((8, LANES), F32),
            vmem((CHIPS, 8, LANES), F32),
            vmem((8, LANES), F32),
            vmem((8, 8, LANES), F32),
            dma((8,)), dma((11,)), dma((2,)), dma((2,)),
            dma((8,)), dma((8,)), dma((8,)), dma((8,)), dma((16,)), dma((16,)), dma((2,)),
            dma((16,)), dma((16,)),
            dma((8,)), dma((16,)), dma((16,)), dma((8,)),
            dma((16,)), dma((8,)), dma((8,)), dma((8,)),
        ],
        compiler_params=pltpu.CompilerParams(
            collective_id=0, has_side_effects=True, vmem_limit_bytes=56 * 2**20
        ),
        cost_estimate=pl.CostEstimate(flops=6 * 10**9, bytes_accessed=7 * 2**20, transcendentals=0),
    )(
        query_branch, key_raw, value_branch, conv_out, out_grad, long_filter, short_filter,
        jnp.asarray(forward), jnp.asarray(inverse),
    )


def solution(mesh):
    both, taps = P("ctx", "ch"), P(None, "ch")
    return jax.shard_map(
        per_device,
        mesh=mesh,
        in_specs=(both,) * 6 + (taps,),
        out_specs=(both,) * 4 + (taps,),
        check_vma=False,
    )
```

time: 763 us -> 62.4 us (0.08)
  other arithmetic: 209 us -> 0 us
  matrix products: 204 us -> 0 us
  blocking collectives: 125 us -> 0 us
  waiting for transfers between devices: 94.6 us -> 0 us
  local copies, waits for them, and re-layouts: 71.7 us -> 5.13 us
  Pallas kernels: 0 us -> 56.4 us
  starting transfers between devices: 36.3 us -> 0 us
  between operations: 15 us -> 0.66 us
    dot_general x17 -> x0, matrix products: 204 us -> none  [the longest x16 198 us: forward(): return jnp.dot(forward_pair, doubled, preferred_element_type=jnp.float32)]
    add x48 -> x0, other arithmetic: 192 us -> none  [the longest x16 83.3 us: pair_step(): out_acc + conj_product(filter_spec + parity * prev_filter, grad_spec, dc_...]
    psum x2 -> x0, blocking collectives: 125 us -> none  [the longest x1 75 us: per_device(): total_squares = lax.psum(squares, ('ctx', 'ch'))]
    all_gather x2 -> x0, waiting for transfers between devices: 93.8 us -> none  [the longest x1 53.5 us: sequence_blocks(): gateds = lax.all_gather(gated, 'ctx', axis=0, tiled=True)]
    pallas_call x0 -> x1, Pallas kernels: none -> 56.4 us  [per_device(): pl.pallas_call(kernel, out_shape=(block, block, block, jax.ShapeDtypeStru...]
    dynamic_slice x32 -> x0, local copies, waits for them, and re-layouts: 36.2 us -> none  [the longest x16 18.1 us: pair_step(): filter_block = lax.dynamic_slice_in_dim(filters, row_start, block_rows, 0)]
    ppermute x17 -> x0, starting transfers between devices: 36.2 us -> none  [shifted(): return lax.ppermute(block, axis, route)]
    while x15 -> x0, local copies, waits for them, and re-layouts: 28 us -> none
  transfers between devices with their start and end apart: 19 -> 0, of which waited for: 2 -> 0; matrix products, arithmetic and copies ran while one was open for 56% -> 0% of each run, Pallas kernels for 0% -> 0%
where the time goes in v1:
time: 62.4 us; the launch traced here: 62.2 us
  Pallas kernels  56.4 us (90%)
  local copies, waits for them, and re-layouts  5.13 us (8%)
  between operations  0.66 us (1%)
    pallas_call x1, Pallas kernels, per_device(): pl.pallas_call(kernel, out_shape=(block, block, block, jax.ShapeDtypeStru...  56.4 us
    unnamed x13, local copies, waits for them, and re-layouts  5.13 us

profile of v1, /device:TPU:1, one launch (start us, length us, event | category | flops | bytes accessed | tf_op | source)
XLA Modules:
  0.0 62.2 jit_solution(9674712613752077044)
XLA Ops:
  0.6 56.4 %shard_map.128 = (bf16[256,1024]{1,0:T(8,128)(2,1)}, bf16[256,1024]{1,0:T(8,128)(2,1)}, bf16[256,1024]{1,0:T(8,128)(2,1)}, f32[256,1024]{1,0:T(8,128)}, f32[3,1024]{1,0:T(4,128)}) custom-call(bf16[256,1024]{1,0:T(8,128)(2,1)} %qb_hbm.1, bf16[256,1024]{1,0:T(8,128)(2,1)} %kr_hbm.1, bf16[256,1024]{1,0:T(8,128)(2,1)} %vb_hbm.1, bf16[256,1024]{1,0:T(8,128)(2,1)} %co_hbm.1, ...), custom_call_target="tpu_custom_call" | custom-call | flops 6000000000 | bytes 7340032 | tf_op jit(solution)/shard_map/pallas_call | solution.py:528
  57.0 0.0 copy-start.2
  57.1 0.0 copy-start.1
  57.1 2.0 %copy.19 = bf16[256,1024]{1,0:T(8,128)(2,1)} copy(bf16[256,1024]{1,0:T(8,128)(2,1)} %get-tuple-element.10) | data formatting | bytes 1048576
  59.0 0.0 copy-done.2
  59.0 0.0 copy-start
  59.0 0.8 %copy.20 = bf16[256,1024]{1,0:T(8,128)(2,1)} copy(bf16[256,1024]{1,0:T(8,128)(2,1)S(1)} %copy-done.2) | data formatting | bytes 1048576
  59.8 0.0 copy-done.1
  59.8 0.8 %copy.21 = bf16[256,1024]{1,0:T(8,128)(2,1)} copy(bf16[256,1024]{1,0:T(8,128)(2,1)S(1)} %copy-done.1) | data formatting | bytes 1048576
  60.6 0.0 copy-done
  60.6 0.0 copy-start.3
  60.6 1.0 %copy.22 = f32[256,1024]{1,0:T(8,128)} copy(f32[256,1024]{1,0:T(8,128)S(1)} %copy-done) | data formatting | bytes 2097152
  61.6 0.0 copy-done.3
  61.6 0.6 copy.23
Async XLA Ops:
  57.0 2.0 %copy-start.2 = (bf16[256,1024]{1,0:T(8,128)(2,1)S(1)}, bf16[256,1024]{1,0:T(8,128)(2,1)}, u32[]{:S(2)}) copy-start(bf16[256,1024]{1,0:T(8,128)(2,1)} %get-tuple-element.11) | copy-start | bytes 1572868
  57.1 2.8 %copy-start.1 = (bf16[256,1024]{1,0:T(8,128)(2,1)S(1)}, bf16[256,1024]{1,0:T(8,128)(2,1)}, u32[]{:S(2)}) copy-start(bf16[256,1024]{1,0:T(8,128)(2,1)} %get-tuple-element.12) | copy-start | bytes 1572868
  59.0 1.6 %copy-start = (f32[256,1024]{1,0:T(8,128)S(1)}, f32[256,1024]{1,0:T(8,128)}, u32[]{:S(2)}) copy-start(f32[256,1024]{1,0:T(8,128)} %get-tuple-element.13) | copy-start | bytes 3145732
  60.6 1.0 %copy-start.3 = (f32[3,1024]{1,0:T(4,128)S(1)}, f32[3,1024]{1,0:T(4,128)}, u32[]{:S(2)}) copy-start(f32[3,1024]{1,0:T(4,128)} %get-tuple-element.14) | copy-start | bytes 36868

commit v2 on v1

v2 whole, which is shorter than its diff:
```python
import functools

import jax
import jax.numpy as jnp
import ml_dtypes
import numpy as np
from jax import lax
from jax.experimental import pallas as pl
from jax.experimental.pallas import tpu as pltpu
from jax.sharding import PartitionSpec as P

MESH = pl.DeviceIdType.MESH
F32, BF16 = jnp.float32, jnp.bfloat16
ROWS, WIDTH, LANES, CHIPS, BLOCKS = 256, 1024, 128, 8, 16
TAPS = 3
FINISH_PARTS = 4
FIRST = 4
AHEAD = 4


def tables():
    length = 2 * ROWS
    rows = np.arange(length)
    freq = np.where(rows <= ROWS, rows, rows - ROWS)
    angle = (freq[:, None] * np.arange(ROWS)[None, :] % length) * (np.pi / ROWS)
    forward = np.where((rows <= ROWS)[:, None], np.cos(angle), -np.sin(angle))
    weight = np.where((freq == 0) | (freq == ROWS), 1.0, 2.0) / length
    inverse = forward.T * weight[None, :]

    def pair(table):
        upper = table.astype(ml_dtypes.bfloat16)
        lower = (table - upper.astype(np.float64)).astype(ml_dtypes.bfloat16)
        return np.concatenate([upper, lower], axis=0)

    return pair(forward), pair(inverse)


def lanes(index):
    return pl.ds(pl.multiple_of(index * LANES, LANES), LANES)


def kernel(
    qb_hbm, kr_hbm, vb_hbm, co_hbm, og_hbm, lf_hbm, taps_ref, fwd_hbm, inv_hbm,
    qg, krg, vg, lag, total_all, short,
    qb, kr, vb, co, og, lf, fwd, inv,
    cg, gated, ext, conv, halo, land, spec_g, sum_g, spec_a, dif_a,
    prod_hi, prod_lo, back, ret, keyg, tail,
    part, pack, pack_land, half_short, half_land, squares, squares_land, total, total_land,
    in_sem, halo_sem, tail_sem, send_sem, come_sem, pass_sem, other_sem, own_sem, rs_sem, rr_sem,
    pack_sem, bs_sem, br_sem, s1s_sem, s1r_sem, s2s_sem, s2r_sem,
):
    me = lax.axis_index("ctx")
    group = lax.axis_index("ch")
    chip, core = me // 2, lax.rem(me, 2)
    sibling = chip * 2 + 1 - core
    chip_x, chip_y = chip // 4, lax.rem(chip, 4)

    def chip_at(step, sign):
        dx, dy = lax.rem(step, 2), step // 2
        return lax.rem(chip_x + dx, 2) * 4 + lax.rem(chip_y + 4 + sign * dy, 4)

    dests = [chip_at(step, 1) for step in range(1, CHIPS)]
    sources = [chip_at(step, -1) for step in range(1, CHIPS)]
    mine, other = lanes(core), lanes(1 - core)

    def remote(src, dst, send, recv, ctx):
        return pltpu.make_async_remote_copy(
            src_ref=src, dst_ref=dst, send_sem=send, recv_sem=recv,
            device_id={"ctx": ctx}, device_id_type=MESH,
        )

    def arrived(ref, sem):
        pltpu.make_async_copy(ref, ref, sem).wait()

    loads = [
        pltpu.make_async_copy(src, dst, in_sem.at[n])
        for n, (src, dst) in enumerate(
            ((og_hbm, og), (qb_hbm, qb), (kr_hbm, kr), (lf_hbm, lf), (vb_hbm, vb),
             (fwd_hbm, fwd), (co_hbm, co), (inv_hbm, inv))
        )
    ]
    for load in loads:
        load.start()
    og_in, qb_in, kr_in, lf_in, vb_in, fwd_in, co_in, inv_in = loads

    barrier = pltpu.get_barrier_semaphore()
    for step in range(1, BLOCKS):
        pl.semaphore_signal(
            barrier, inc=1, device_id={"ctx": lax.rem(me + step, BLOCKS)}, device_id_type=MESH
        )
    for step in range(1, 8):
        pl.semaphore_signal(
            barrier, inc=1, device_id={"ch": lax.rem(group + step, 8)}, device_id_type=MESH
        )

    og_in.wait()
    qb_in.wait()

    def make_grad(p, carry):
        at = lanes(p)
        cg[:, at] = (og[:, at].astype(F32) * qb[:, at].astype(F32)).astype(BF16)
        return carry

    lax.fori_loop(0, CHIPS, make_grad, 0)
    kr_in.wait()
    lf_in.wait()
    pl.semaphore_wait(barrier, BLOCKS - 1 + 7)

    def halo_copy():
        return remote(
            kr.at[pl.ds(ROWS - 16, 16)], halo, halo_sem.at[0], halo_sem.at[1],
            lax.rem(me + 1, BLOCKS),
        )

    @pl.when(me < BLOCKS - 1)
    def _():
        halo_copy().start()

    def send_out(kind, block):
        copies = []
        for n, p in enumerate([chip] + dests):
            own = n == 0
            copies.append(
                remote(
                    block.at[:, lanes(p)], land.at[kind, chip, :, mine], send_sem.at[kind, n],
                    other_sem.at[kind, chip] if own else come_sem.at[kind, chip],
                    sibling if own else p * 2 + core,
                )
            )
            copies[-1].start()
        keep = pltpu.make_async_copy(
            block.at[:, lanes(chip)], land.at[kind, chip, :, mine], own_sem.at[kind]
        )
        keep.start()
        return copies, keep

    grad_sends, grad_keep = send_out(0, cg)
    filter_sends, filter_keep = send_out(1, lf)

    vb_in.wait()

    @pl.when(me > 0)
    def _():
        arrived(halo, halo_sem.at[1])
        ext[0:8, :] = halo[...].astype(F32)[8:16]

    @pl.when(me == 0)
    def _():
        ext[0:8, :] = jnp.zeros((8, WIDTH), F32)

    def make_gated(p, carry):
        at = lanes(p)
        ext[8:, at] = kr[:, at].astype(F32)
        value = jnp.zeros((ROWS, LANES), F32)
        for j in range(TAPS):
            value = value + taps_ref[j : j + 1, at] * ext[8 - j : 8 - j + ROWS, at]
        conv[:, at] = value
        gated[:, at] = (value * vb[:, at].astype(F32)).astype(BF16)
        return carry

    lax.fori_loop(0, CHIPS, make_gated, 0)
    gated_sends, gated_keep = send_out(2, gated)
    co_in.wait()

    def make_query(p, carry):
        at = lanes(p)
        qg[:, at] = (og[:, at].astype(F32) * co[:, at].astype(F32)).astype(BF16)
        return carry

    lax.fori_loop(0, CHIPS, make_query, 0)

    fwd_in.wait()

    def transform(block):
        upper = jnp.dot(fwd[: 2 * ROWS], block, preferred_element_type=F32)
        return upper + jnp.dot(fwd[2 * ROWS :], block, preferred_element_type=F32)

    def spectra(kind, keep, put):
        def pair(source):
            arrived(land.at[kind, source, :, other], other_sem.at[kind, source])
            put(source, transform(land[kind, source]))

        def handed(step):
            source = chip_at(step, -1)
            block = land.at[kind, source, :, mine]
            return remote(
                block, block, pass_sem.at[kind, step], other_sem.at[kind, source], sibling
            )

        def hand(step):
            source = chip_at(step, -1)
            arrived(land.at[kind, source, :, mine], come_sem.at[kind, source])
            handed(step).start()

        def turn(step, carry):
            @pl.when(step < CHIPS)
            def _():
                hand(step)

            pair(chip_at(step - AHEAD, -1))
            return carry

        keep.wait()
        for step in range(1, AHEAD):
            hand(step)
        lax.fori_loop(AHEAD, CHIPS + AHEAD, turn, 0)
        return [handed(step) for step in range(1, CHIPS)]

    def put_grad(source, value):
        spec_g[source] = value

    def put_other(source, value):
        spec_a[source] = value
        dif_a[source] = value[:ROWS] - value[ROWS:]

    handed = spectra(0, grad_keep, put_grad)
    spec_g[CHIPS] = jnp.zeros((2 * ROWS, 2 * LANES), F32)

    def join_from(first):
        def join(m, carry):
            even = (lax.broadcasted_iota(jnp.int32, (2 * ROWS, LANES), 0) % 2) == 0
            for n in range(2):
                now, later = first + n, first + n + 1
                a = spec_g[m + now // 2, :, now % 2 * LANES : (now % 2 + 1) * LANES]
                b = spec_g[m + later // 2, :, later % 2 * LANES : (later % 2 + 1) * LANES]
                value = a + jnp.where(even, b, -b)
                at = slice(n * LANES, (n + 1) * LANES)
                spec_g[m, :, at] = value
                sum_g[m, :, at] = value[:ROWS] + value[ROWS:]
            return carry

        lax.fori_loop(0, CHIPS, join, 0)

    @pl.when(core == 0)
    def _():
        join_from(0)

    @pl.when(core == 1)
    def _():
        join_from(1)

    def products(chunk, carry):
        for base in (0, 8):
            halves = []
            for sub in range(2):
                row = pl.multiple_of(chunk * 16 + sub * 8, 8)
                re_at, im_at = pl.ds(row, 8), pl.ds(pl.multiple_of(row + ROWS, 8), 8)
                real, both, cross, held = [None] * 4, [None] * 4, [None] * 4, []
                for m in range(base, BLOCKS):
                    at = slice((m % 2) * LANES, (m % 2 + 1) * LANES)
                    g_re, g_im = spec_g[m // 2, re_at, at], spec_g[m // 2, im_at, at]
                    g_sum = sum_g[m // 2, re_at, at]
                    j = m - base
                    at = slice((j % 2) * LANES, (j % 2 + 1) * LANES)
                    held.append(
                        (spec_a[j // 2, re_at, at], spec_a[j // 2, im_at, at], dif_a[j // 2, re_at, at])
                    )
                    for u in range(min(4, j // 2 + 1)):
                        a_re, a_im, a_dif = held[j - 2 * u]
                        terms = (a_re * g_re, a_im * g_im, a_dif * g_sum)
                        for sums, term in zip((real, both, cross), terms):
                            sums[u] = term if sums[u] is None else sums[u] + term
                edge = (lax.broadcasted_iota(jnp.int32, (8, LANES), 0) + row) == 0
                halves.append(
                    [
                        (
                            jnp.where(edge, real[u], real[u] + both[u]),
                            jnp.where(edge, both[u], cross[u] - real[u] + both[u]),
                        )
                        for u in range(4)
                    ]
                )
            start = pl.multiple_of(chunk * 16, 16)
            for u in range(4):
                at = slice((base // 2 + u) * LANES, (base // 2 + u + 1) * LANES)
                for which, offset in ((0, 0), (1, ROWS)):
                    value = jnp.concatenate([halves[0][u][which], halves[1][u][which]], axis=0)
                    upper = value.astype(BF16)
                    rows_at = pl.ds(pl.multiple_of(start + offset, 16), 16)
                    prod_hi[rows_at, at] = upper
                    prod_lo[rows_at, at] = (value - upper.astype(F32)).astype(BF16)
        return carry

    def restore(kind):
        twice = jnp.dot(inv[...], prod_hi[...], preferred_element_type=F32)
        result = twice[:ROWS] + twice[ROWS:]
        result = result + jnp.dot(inv[:ROWS], prod_lo[...], preferred_element_type=F32)
        for k in range(CHIPS // 2):
            back[kind, k] = result[:, k * 2 * LANES : (k + 1) * 2 * LANES].astype(BF16)
        if kind == 1:
            square = result * result
            square = sum(square[:, k * LANES : (k + 1) * LANES] for k in range(CHIPS))
            squares[...] = jnp.sum(square.reshape(ROWS // 8, 8, LANES), axis=0)

    def give_back(kind, n, p, goal):
        copy = remote(
            back.at[kind, p // 2, :, lanes(lax.rem(p, 2))], goal.at[:, lanes(chip)],
            rs_sem.at[kind, n], rr_sem.at[kind, chip], p * 2 + core,
        )
        copy.start()
        return copy

    def keep_back(kind, goal):
        copy = pltpu.make_async_copy(
            back.at[kind, chip // 2, :, lanes(lax.rem(chip, 2))], goal.at[:, lanes(chip)],
            own_sem.at[3 + kind],
        )
        copy.start()
        return copy

    handed = handed + spectra(1, filter_keep, put_other)
    lax.fori_loop(0, ROWS // 16, products, 0)
    inv_in.wait()
    restore(0)
    returns = [give_back(0, n, p, ret) for n, p in enumerate(dests)]
    ret_keep = keep_back(0, ret)

    handed = handed + spectra(2, gated_keep, put_other)
    lax.fori_loop(0, ROWS // 16, products, 0)
    restore(1)

    square_sends = []
    for step in range(1, BLOCKS):
        copy = remote(
            squares, squares_land.at[me], s1s_sem.at[step], s1r_sem.at[me],
            lax.rem(me + step, BLOCKS),
        )
        copy.start()
        square_sends.append(copy)
    squares_land[me] = squares[...]
    returns += [give_back(1, n, p, lag) for n, p in enumerate(dests[:FIRST])]
    lag_keep = keep_back(1, lag)

    part[...] = jnp.zeros((8, WIDTH), F32)

    def branch(source):
        at = lanes(source)
        wide = ret[:, at].astype(F32)
        vg[:, at] = (wide * conv[:, at]).astype(BF16)
        key = wide * vb[:, at].astype(F32)
        keyg[0:ROWS, at] = key
        for j in range(TAPS):
            part[j : j + 1, at] = jnp.sum(key * ext[8 - j : 8 - j + ROWS, at], axis=0, keepdims=True)

    def branch_turn(step, carry):
        source = chip_at(step, -1)
        arrived(ret.at[:, lanes(source)], rr_sem.at[0, source])
        branch(source)
        return carry

    ret_keep.wait()
    branch(chip)
    lax.fori_loop(1, CHIPS, branch_turn, 0)

    def tail_copy():
        return remote(
            keyg.at[pl.ds(0, 8)], tail, tail_sem.at[0], tail_sem.at[1],
            lax.rem(me + BLOCKS - 1, BLOCKS),
        )

    @pl.when(me > 0)
    def _():
        tail_copy().start()

    for p in range(CHIPS):
        pack[p * TAPS : (p + 1) * TAPS, :] = part[0:TAPS, p * LANES : (p + 1) * LANES]
    pack_sends = []
    for n, p in enumerate(dests):
        copy = remote(pack, pack_land.at[chip], bs_sem.at[n], br_sem.at[chip], p * 2 + core)
        copy.start()
        pack_sends.append(copy)
    pack_land[chip] = pack[...]
    returns += [give_back(1, n + FIRST, p, lag) for n, p in enumerate(dests[FIRST:])]

    for step in range(1, BLOCKS):
        source = lax.rem(me + BLOCKS - step, BLOCKS)
        arrived(squares_land.at[source], s1r_sem.at[source])
    total[...] = jnp.sum(squares_land[...], axis=0)
    total_sends = []
    for step in range(1, 8):
        copy = pltpu.make_async_remote_copy(
            src_ref=total, dst_ref=total_land.at[group], send_sem=s2s_sem.at[step],
            recv_sem=s2r_sem.at[group], device_id={"ch": lax.rem(group + step, 8)},
            device_id_type=MESH,
        )
        copy.start()
        total_sends.append(copy)
    total_land[group] = total[...]

    @pl.when(me < BLOCKS - 1)
    def _():
        arrived(tail, tail_sem.at[1])
        keyg[ROWS : ROWS + 8, :] = tail[...]

    @pl.when(me == BLOCKS - 1)
    def _():
        keyg[ROWS : ROWS + 8, :] = jnp.zeros((8, WIDTH), F32)

    def make_raw(p, carry):
        at = lanes(p)
        value = jnp.zeros((ROWS, LANES), F32)
        for j in range(TAPS):
            value = value + taps_ref[j : j + 1, at] * keyg[j : j + ROWS, at]
        krg[:, at] = value.astype(BF16)
        return carry

    lax.fori_loop(0, CHIPS, make_raw, 0)

    for source in sources:
        arrived(pack_land.at[source], br_sem.at[source])
    half_short[...] = jnp.sum(pack_land[...], axis=0)
    swap = remote(half_short, half_land, pack_sem.at[0], pack_sem.at[1], sibling)
    swap.start()
    for step in range(1, 8):
        source = lax.rem(group + 8 - step, 8)
        arrived(total_land.at[source], s2r_sem.at[source])
    total_all[...] = jnp.sum(total_land[...], axis=0)
    swap.wait()
    short[...] = half_short[...] + half_land[...]
    lag_keep.wait()
    for source in sources:
        arrived(lag.at[:, lanes(source)], rr_sem.at[1, source])

    for copies in (grad_sends, filter_sends, gated_sends, handed, returns):
        for copy in copies:
            copy.wait_send()
    for copies in (square_sends, pack_sends, total_sends):
        for copy in copies:
            copy.wait_send()

    @pl.when(me < BLOCKS - 1)
    def _():
        halo_copy().wait_send()

    @pl.when(me > 0)
    def _():
        tail_copy().wait_send()


def finish(qg, krg, vg, lag, total, short, qg_out, krg_out, vg_out, fg_out, sg_out, fg, sems):
    copies = [
        pltpu.make_async_copy(src, dst, sems.at[n])
        for n, (src, dst) in enumerate(((qg, qg_out), (krg, krg_out), (vg, vg_out)))
    ]
    for copy in copies:
        copy.start()
    everything = jnp.sum(total[...], axis=(0, 1), keepdims=True)
    scale = lax.rsqrt(everything / float(4096 * 8192) + 1e-06)
    rows = ROWS // FINISH_PARTS
    for n in range(FINISH_PARTS):
        at = pl.ds(n * rows, rows)
        fg[at, :] = lag[at, :].astype(F32) * scale
        copy = pltpu.make_async_copy(fg.at[at], fg_out.at[at], sems.at[3 + n])
        copy.start()
        copies.append(copy)
    for p in range(CHIPS):
        sg_out[:, p * LANES : (p + 1) * LANES] = short[p * TAPS : (p + 1) * TAPS, :]
    for copy in copies:
        copy.wait()


def per_device(query_branch, key_raw, value_branch, conv_out, out_grad, long_filter, short_filter):
    forward, inverse = tables()
    anywhere = pl.BlockSpec(memory_space=pl.ANY)
    in_hbm = pl.BlockSpec(memory_space=pltpu.HBM)
    in_vmem = pl.BlockSpec(memory_space=pltpu.VMEM)
    block = jax.ShapeDtypeStruct((ROWS, WIDTH), BF16)
    dma = pltpu.SemaphoreType.DMA
    vmem = pltpu.VMEM
    results = pl.pallas_call(
        kernel,
        out_shape=(
            *[vmem((ROWS, WIDTH), BF16)] * 4,
            vmem((8, LANES), F32),
            vmem((CHIPS * TAPS, LANES), F32),
        ),
        in_specs=[in_hbm] * 6 + [in_vmem] + [in_hbm] * 2,
        out_specs=(in_vmem,) * 6,
        scratch_shapes=[
            *[vmem((ROWS, WIDTH), BF16)] * 6,
            vmem((4 * ROWS, ROWS), BF16),
            vmem((2 * ROWS, 2 * ROWS), BF16),
            vmem((ROWS, WIDTH), BF16),
            vmem((ROWS, WIDTH), BF16),
            vmem((ROWS + 8, WIDTH), F32),
            vmem((ROWS, WIDTH), F32),
            vmem((16, WIDTH), BF16),
            vmem((3, CHIPS, ROWS, 2 * LANES), BF16),
            vmem((CHIPS + 1, 2 * ROWS, 2 * LANES), F32),
            vmem((CHIPS, ROWS, 2 * LANES), F32),
            vmem((CHIPS, 2 * ROWS, 2 * LANES), F32),
            vmem((CHIPS, ROWS, 2 * LANES), F32),
            vmem((2 * ROWS, CHIPS * LANES), BF16),
            vmem((2 * ROWS, CHIPS * LANES), BF16),
            vmem((2, CHIPS // 2, ROWS, 2 * LANES), BF16),
            vmem((ROWS, WIDTH), BF16),
            vmem((ROWS + 8, WIDTH), F32),
            vmem((8, WIDTH), F32),
            vmem((8, WIDTH), F32),
            vmem((CHIPS * TAPS, LANES), F32),
            vmem((CHIPS, CHIPS * TAPS, LANES), F32),
            vmem((CHIPS * TAPS, LANES), F32),
            vmem((CHIPS * TAPS, LANES), F32),
            vmem((8, LANES), F32),
            vmem((BLOCKS, 8, LANES), F32),
            vmem((8, LANES), F32),
            vmem((8, 8, LANES), F32),
            dma((8,)), dma((2,)), dma((2,)), dma((3, 8)), dma((3, 8)), dma((3, 8)), dma((3, 8)),
            dma((5,)), dma((2, 8)), dma((2, 8)),
            dma((2,)), dma((8,)), dma((8,)), dma((16,)), dma((16,)), dma((8,)), dma((8,)),
        ],
        compiler_params=pltpu.CompilerParams(
            collective_id=0, has_side_effects=True, vmem_limit_bytes=61 * 2**20
        ),
        cost_estimate=pl.CostEstimate(flops=6 * 10**9, bytes_accessed=7 * 2**20, transcendentals=0),
    )(
        query_branch, key_raw, value_branch, conv_out, out_grad, long_filter, short_filter,
        jnp.asarray(forward), jnp.asarray(inverse),
    )
    return pl.pallas_call(
        finish,
        out_shape=(
            block, block, block,
            jax.ShapeDtypeStruct((ROWS, WIDTH), F32),
            jax.ShapeDtypeStruct((TAPS, WIDTH), F32),
        ),
        in_specs=[in_vmem] * 6,
        out_specs=(anywhere, anywhere, anywhere, anywhere, in_vmem),
        scratch_shapes=[vmem((ROWS, WIDTH), F32), dma((3 + FINISH_PARTS,))],
        compiler_params=pltpu.CompilerParams(vmem_limit_bytes=8 * 2**20),
    )(*results)


def solution(mesh):
    both, taps = P("ctx", "ch"), P(None, "ch")
    return jax.shard_map(
        per_device,
        mesh=mesh,
        in_specs=(both,) * 6 + (taps,),
        out_specs=(both,) * 4 + (taps,),
        check_vma=False,
    )
```

time: 62.4 us -> 52.8 us (0.85)
  local copies, waits for them, and re-layouts: 5.13 us -> 0 us
  Pallas kernels: 56.4 us -> 52 us
    unnamed x13 -> x0, local copies, waits for them, and re-layouts: 5.13 us -> none
    pallas_call x1 -> x2, Pallas kernels: 56.4 us -> 52 us  [the longest x1 49.8 us: per_device(): pl.pallas_call(kernel, out_shape=(*[vmem((ROWS, WIDTH), BF16)] * 4, vmem(...]
where the time goes in v2:
time: 52.8 us; the launch traced here: 52.6 us
  Pallas kernels  52 us (98%)
  between operations  0.64 us (1%)
    pallas_call x1, Pallas kernels, per_device(): pl.pallas_call(kernel, out_shape=(*[vmem((ROWS, WIDTH), BF16)] * 4, vmem(...  49.8 us
    pallas_call x1, Pallas kernels, per_device(): pl.pallas_call(finish, out_shape=(block, block, block, jax.ShapeDtypeStru...  2.15 us

profile of v2, /device:TPU:1, one launch (start us, length us, event | category | flops | bytes accessed | tf_op | source)
XLA Modules:
  0.0 52.6 jit_solution(9861103592578491491)
XLA Ops:
  0.6 49.8 %shard_map.128 = (bf16[256,1024]{1,0:T(8,128)(2,1)S(1)}, bf16[256,1024]{1,0:T(8,128)(2,1)S(1)}, bf16[256,1024]{1,0:T(8,128)(2,1)S(1)}, bf16[256,1024]{1,0:T(8,12...) custom-call(bf16[256,1024]{1,0:T(8,128)(2,1)} %qb_hbm.1, bf16[256,1024]{1,0:T(8,128)(2,1)} %kr_hbm.1, ...), custom_call_target="tpu_custom_call" | custom-call | flops 6000000000 | bytes 7340032 | tf_op jit(solution)/shard_map/pallas_call | solution.py:470
  50.5 2.1 %shard_map.129 = (bf16[256,1024]{1,0:T(8,128)(2,1)}, bf16[256,1024]{1,0:T(8,128)(2,1)}, bf16[256,1024]{1,0:T(8,128)(2,1)}, f32[256,1024]{1,0:T(8,128)}, f32[3,1024]{1,0:T(4,128)}) custom-call(bf16[256,1024]{1,0:T(8,128)(2,1)S(1)} %get-tuple-element.11.qg, bf16[256,1024]{1,0:T(8,128)(2,1)S(1)} %get-tuple-element.12.krg, ...), custom_call_target="tpu_custom_call" | custom-call | tf_op jit(solution)/shard_map/pallas_call | solution.py:520

commit v3 on v2

--- a/solution.py
+++ b/solution.py
@@ -14,8 +14,7 @@
 ROWS, WIDTH, LANES, CHIPS, BLOCKS = 256, 1024, 128, 8, 16
 TAPS = 3
 FINISH_PARTS = 4
-FIRST = 4
-AHEAD = 4
+AHEAD = 3
 
 
 def tables():
@@ -172,10 +171,10 @@
     fwd_in.wait()
 
     def transform(block):
-        upper = jnp.dot(fwd[: 2 * ROWS], block, preferred_element_type=F32)
-        return upper + jnp.dot(fwd[2 * ROWS :], block, preferred_element_type=F32)
-
-    def spectra(kind, keep, put):
+        twice = jnp.dot(fwd[...], block, preferred_element_type=F32)
+        return twice[: 2 * ROWS] + twice[2 * ROWS :]
+
+    def spectra(kind, keep, put, begin=False, begun=False):
         def pair(source):
             arrived(land.at[kind, source, :, other], other_sem.at[kind, source])
             put(source, transform(land[kind, source]))
@@ -200,9 +199,12 @@
             pair(chip_at(step - AHEAD, -1))
             return carry
 
-        keep.wait()
-        for step in range(1, AHEAD):
-            hand(step)
+        if not begun:
+            keep.wait()
+            for step in range(1, AHEAD):
+                hand(step)
+        if begin:
+            return None
         lax.fori_loop(AHEAD, CHIPS + AHEAD, turn, 0)
         return [handed(step) for step in range(1, CHIPS)]
 
@@ -239,8 +241,10 @@
     def _():
         join_from(1)
 
-    def products(chunk, carry):
-        for base in (0, 8):
+    def products(half):
+        base = 2 * half
+
+        def turn(chunk, carry):
             halves = []
             for sub in range(2):
                 row = pl.multiple_of(chunk * 16 + sub * 8, 8)
@@ -255,8 +259,8 @@
                     held.append(
                         (spec_a[j // 2, re_at, at], spec_a[j // 2, im_at, at], dif_a[j // 2, re_at, at])
                     )
-                    for u in range(min(4, j // 2 + 1)):
-                        a_re, a_im, a_dif = held[j - 2 * u]
+                    for u in range(min(4, j // 4 + 1)):
+                        a_re, a_im, a_dif = held[j - 4 * u]
                         terms = (a_re * g_re, a_im * g_im, a_dif * g_sum)
                         for sums, term in zip((real, both, cross), terms):
                             sums[u] = term if sums[u] is None else sums[u] + term
@@ -272,52 +276,78 @@
                 )
             start = pl.multiple_of(chunk * 16, 16)
             for u in range(4):
-                at = slice((base // 2 + u) * LANES, (base // 2 + u + 1) * LANES)
+                at = slice((half * 4 + u) * LANES, (half * 4 + u + 1) * LANES)
                 for which, offset in ((0, 0), (1, ROWS)):
                     value = jnp.concatenate([halves[0][u][which], halves[1][u][which]], axis=0)
                     upper = value.astype(BF16)
                     rows_at = pl.ds(pl.multiple_of(start + offset, 16), 16)
                     prod_hi[rows_at, at] = upper
                     prod_lo[rows_at, at] = (value - upper.astype(F32)).astype(BF16)
-        return carry
-
-    def restore(kind):
-        twice = jnp.dot(inv[...], prod_hi[...], preferred_element_type=F32)
+            return carry
+
+        lax.fori_loop(0, ROWS // 16, turn, 0)
+
+    def restore(kind, half):
+        at = slice(half * 4 * LANES, (half + 1) * 4 * LANES)
+        twice = jnp.dot(inv[...], prod_hi[:, at], preferred_element_type=F32)
         result = twice[:ROWS] + twice[ROWS:]
-        result = result + jnp.dot(inv[:ROWS], prod_lo[...], preferred_element_type=F32)
-        for k in range(CHIPS // 2):
-            back[kind, k] = result[:, k * 2 * LANES : (k + 1) * 2 * LANES].astype(BF16)
+        result = result + jnp.dot(inv[:ROWS], prod_lo[:, at], preferred_element_type=F32)
+        for k in range(2):
+            back[kind, half * 2 + k] = result[:, k * 2 * LANES : (k + 1) * 2 * LANES].astype(BF16)
         if kind == 1:
             square = result * result
-            square = sum(square[:, k * LANES : (k + 1) * LANES] for k in range(CHIPS))
-            squares[...] = jnp.sum(square.reshape(ROWS // 8, 8, LANES), axis=0)
-
-    def give_back(kind, n, p, goal):
-        copy = remote(
-            back.at[kind, p // 2, :, lanes(lax.rem(p, 2))], goal.at[:, lanes(chip)],
-            rs_sem.at[kind, n], rr_sem.at[kind, chip], p * 2 + core,
-        )
-        copy.start()
-        return copy
+            square = sum(square[:, k * LANES : (k + 1) * LANES] for k in range(4))
+            squares[...] += jnp.sum(square.reshape(ROWS // 8, 8, LANES), axis=0)
+
+    def back_copy(kind, half, step, goal):
+        p = lax.rem(chip_x + step, 2) * 4 + lax.rem(chip_y // 2 + step // 2, 2) * 2 + half
+        return remote(
+            back.at[kind, half * 2 + p // 4, :, lanes(lax.rem(p, 4) // 2)], goal.at[:, lanes(chip)],
+            rs_sem.at[kind, half * 4 + step], rr_sem.at[kind, chip], p * 2 + core,
+        )
 
     def keep_back(kind, goal):
-        copy = pltpu.make_async_copy(
-            back.at[kind, chip // 2, :, lanes(lax.rem(chip, 2))], goal.at[:, lanes(chip)],
+        return pltpu.make_async_copy(
+            back.at[kind, lax.rem(chip, 2) * 2 + chip // 4, :, lanes(lax.rem(chip, 4) // 2)], goal.at[:, lanes(chip)],
             own_sem.at[3 + kind],
         )
-        copy.start()
-        return copy
+
+    def give_back(kind, half, goal):
+        for step in range(1, 4):
+            back_copy(kind, half, step, goal).start()
+
+        @pl.when(lax.rem(chip, 2) != half)
+        def _():
+            back_copy(kind, half, 0, goal).start()
+
+        @pl.when(lax.rem(chip, 2) == half)
+        def _():
+            keep_back(kind, goal).start()
+
+    def given_back(kind, half, goal):
+        for step in range(1, 4):
+            back_copy(kind, half, step, goal).wait_send()
+
+        @pl.when(lax.rem(chip, 2) != half)
+        def _():
+            back_copy(kind, half, 0, goal).wait_send()
 
     handed = handed + spectra(1, filter_keep, put_other)
-    lax.fori_loop(0, ROWS // 16, products, 0)
     inv_in.wait()
-    restore(0)
-    returns = [give_back(0, n, p, ret) for n, p in enumerate(dests)]
-    ret_keep = keep_back(0, ret)
-
-    handed = handed + spectra(2, gated_keep, put_other)
-    lax.fori_loop(0, ROWS // 16, products, 0)
-    restore(1)
+    for half in (1, 0):
+        products(half)
+        restore(0, half)
+        give_back(0, half, ret)
+        if half == 1:
+            spectra(2, gated_keep, put_other, begin=True)
+
+    handed = handed + spectra(2, gated_keep, put_other, begun=True)
+    squares[...] = jnp.zeros((8, LANES), F32)
+    products(1)
+    restore(1, 1)
+    give_back(1, 1, lag)
+    products(0)
+    restore(1, 0)
 
     square_sends = []
     for step in range(1, BLOCKS):
@@ -328,8 +358,6 @@
         copy.start()
         square_sends.append(copy)
     squares_land[me] = squares[...]
-    returns += [give_back(1, n, p, lag) for n, p in enumerate(dests[:FIRST])]
-    lag_keep = keep_back(1, lag)
 
     part[...] = jnp.zeros((8, WIDTH), F32)
 
@@ -348,7 +376,7 @@
         branch(source)
         return carry
 
-    ret_keep.wait()
+    keep_back(0, ret).wait()
     branch(chip)
     lax.fori_loop(1, CHIPS, branch_turn, 0)
 
@@ -370,7 +398,20 @@
         copy.start()
         pack_sends.append(copy)
     pack_land[chip] = pack[...]
-    returns += [give_back(1, n + FIRST, p, lag) for n, p in enumerate(dests[FIRST:])]
+    give_back(1, 0, lag)
+
+    def make_raw(start, rows):
+        def turn(p, carry):
+            at = lanes(p)
+            value = jnp.zeros((rows, LANES), F32)
+            for j in range(TAPS):
+                value = value + taps_ref[j : j + 1, at] * keyg[start + j : start + j + rows, at]
+            krg[start : start + rows, at] = value.astype(BF16)
+            return carry
+
+        return turn
+
+    lax.fori_loop(0, CHIPS, make_raw(0, ROWS - 16), 0)
 
     for step in range(1, BLOCKS):
         source = lax.rem(me + BLOCKS - step, BLOCKS)
@@ -396,15 +437,7 @@
     def _():
         keyg[ROWS : ROWS + 8, :] = jnp.zeros((8, WIDTH), F32)
 
-    def make_raw(p, carry):
-        at = lanes(p)
-        value = jnp.zeros((ROWS, LANES), F32)
-        for j in range(TAPS):
-            value = value + taps_ref[j : j + 1, at] * keyg[j : j + ROWS, at]
-        krg[:, at] = value.astype(BF16)
-        return carry
-
-    lax.fori_loop(0, CHIPS, make_raw, 0)
+    lax.fori_loop(0, CHIPS, make_raw(ROWS - 16, 16), 0)
 
     for source in sources:
         arrived(pack_land.at[source], br_sem.at[source])
@@ -417,16 +450,20 @@
     total_all[...] = jnp.sum(total_land[...], axis=0)
     swap.wait()
     short[...] = half_short[...] + half_land[...]
-    lag_keep.wait()
+    keep_back(1, lag).wait()
     for source in sources:
         arrived(lag.at[:, lanes(source)], rr_sem.at[1, source])
 
-    for copies in (grad_sends, filter_sends, gated_sends, handed, returns):
+    for copies in (grad_sends, filter_sends, gated_sends, handed):
         for copy in copies:
             copy.wait_send()
     for copies in (square_sends, pack_sends, total_sends):
         for copy in copies:
             copy.wait_send()
+
+    for half in range(2):
+        given_back(0, half, ret)
+        given_back(1, half, lag)
 
     @pl.when(me < BLOCKS - 1)
     def _():

time: 52.8 us -> 51.7 us (0.979)
  Pallas kernels: 52 us -> 50.9 us
    pallas_call x1, Pallas kernels: 49.8 us -> 48.7 us  [per_device(): pl.pallas_call(kernel, out_shape=(*[vmem((ROWS, WIDTH), BF16)] * 4, vmem(...]
where the time goes in v3:
time: 51.7 us; the launch traced here: 51.5 us
  Pallas kernels  50.9 us (98%)
  between operations  0.64 us (1%)
    pallas_call x1, Pallas kernels, per_device(): pl.pallas_call(kernel, out_shape=(*[vmem((ROWS, WIDTH), BF16)] * 4, vmem(...  48.7 us
    pallas_call x1, Pallas kernels, per_device(): pl.pallas_call(finish, out_shape=(block, block, block, jax.ShapeDtypeStru...  2.15 us

profile of v3, /device:TPU:1, one launch (start us, length us, event | category | flops | bytes accessed | tf_op | source)
XLA Modules:
  0.0 51.5 jit_solution(12785279550237859017)
XLA Ops:
  0.6 48.7 %shard_map.128 = (bf16[256,1024]{1,0:T(8,128)(2,1)S(1)}, bf16[256,1024]{1,0:T(8,128)(2,1)S(1)}, bf16[256,1024]{1,0:T(8,128)(2,1)S(1)}, bf16[256,1024]{1,0:T(8,12...) custom-call(bf16[256,1024]{1,0:T(8,128)(2,1)} %qb_hbm.1, bf16[256,1024]{1,0:T(8,128)(2,1)} %kr_hbm.1, ...), custom_call_target="tpu_custom_call" | custom-call | flops 6000000000 | bytes 7340032 | tf_op jit(solution)/shard_map/pallas_call | solution.py:507
  49.4 2.1 %shard_map.129 = (bf16[256,1024]{1,0:T(8,128)(2,1)}, bf16[256,1024]{1,0:T(8,128)(2,1)}, bf16[256,1024]{1,0:T(8,128)(2,1)}, f32[256,1024]{1,0:T(8,128)}, f32[3,1024]{1,0:T(4,128)}) custom-call(bf16[256,1024]{1,0:T(8,128)(2,1)S(1)} %get-tuple-element.11.qg, bf16[256,1024]{1,0:T(8,128)(2,1)S(1)} %get-tuple-element.12.krg, ...), custom_call_target="tpu_custom_call" | custom-call | tf_op jit(solution)/shard_map/pallas_call | solution.py:557

commit v4 on v3

--- a/solution.py
+++ b/solution.py
@@ -217,6 +217,8 @@
 
     handed = spectra(0, grad_keep, put_grad)
     spec_g[CHIPS] = jnp.zeros((2 * ROWS, 2 * LANES), F32)
+
+    spectra(1, filter_keep, put_other, begin=True)
 
     def join_from(first):
         def join(m, carry):
@@ -332,7 +334,7 @@
         def _():
             back_copy(kind, half, 0, goal).wait_send()
 
-    handed = handed + spectra(1, filter_keep, put_other)
+    handed = handed + spectra(1, filter_keep, put_other, begun=True)
     inv_in.wait()
     for half in (1, 0):
         products(half)

time: 51.7 us -> 51.1 us (0.988)
  Pallas kernels: 50.9 us -> 49.9 us
    pallas_call x1, Pallas kernels: 48.7 us -> 47.7 us  [per_device(): pl.pallas_call(kernel, out_shape=(*[vmem((ROWS, WIDTH), BF16)] * 4, vmem(...]
where the time goes in v4:
time: 51.1 us; the launch traced here: 50.5 us
  Pallas kernels  49.9 us (98%)
  between operations  0.64 us (1%)
    pallas_call x1, Pallas kernels, per_device(): pl.pallas_call(kernel, out_shape=(*[vmem((ROWS, WIDTH), BF16)] * 4, vmem(...  47.7 us
    pallas_call x1, Pallas kernels, per_device(): pl.pallas_call(finish, out_shape=(block, block, block, jax.ShapeDtypeStru...  2.15 us

profile of v4, /device:TPU:1, one launch (start us, length us, event | category | flops | bytes accessed | tf_op | source)
XLA Modules:
  0.0 50.5 jit_solution(7798201212332546567)
XLA Ops:
  0.6 47.7 %shard_map.128 = (bf16[256,1024]{1,0:T(8,128)(2,1)S(1)}, bf16[256,1024]{1,0:T(8,128)(2,1)S(1)}, bf16[256,1024]{1,0:T(8,128)(2,1)S(1)}, bf16[256,1024]{1,0:T(8,12...) custom-call(bf16[256,1024]{1,0:T(8,128)(2,1)} %qb_hbm.1, bf16[256,1024]{1,0:T(8,128)(2,1)} %kr_hbm.1, ...), custom_call_target="tpu_custom_call" | custom-call | flops 6000000000 | bytes 7340032 | tf_op jit(solution)/shard_map/pallas_call | solution.py:509
  48.4 2.1 %shard_map.129 = (bf16[256,1024]{1,0:T(8,128)(2,1)}, bf16[256,1024]{1,0:T(8,128)(2,1)}, bf16[256,1024]{1,0:T(8,128)(2,1)}, f32[256,1024]{1,0:T(8,128)}, f32[3,1024]{1,0:T(4,128)}) custom-call(bf16[256,1024]{1,0:T(8,128)(2,1)S(1)} %get-tuple-element.11.qg, bf16[256,1024]{1,0:T(8,128)(2,1)S(1)} %get-tuple-element.12.krg, ...), custom_call_target="tpu_custom_call" | custom-call | tf_op jit(solution)/shard_map/pallas_call | solution.py:559
